TPU v7x, 32 devices: a whole 2x2x4 slice. The times are simulated.
32 devices in a mesh: fsdp: 8 (over z, x), tp: 4 (over y, core).
Axes of the slice: x: 2, y: 2, z: 4, core: 2. Of those that a mesh axis runs over, the one named last changes fastest.
Arguments:
- patch_embeddings: bfloat16 [2, 6400, 768], P(None, ('fsdp', 'tp')), may hold values from -6 to 6
- upstream_gradient: bfloat16 [2, 6400, 768], P(None, ('fsdp', 'tp')), may hold values from -6 to 6
- picture_valid_count: int32 [2, 32], P(None, 'fsdp'), may hold values from 147 to 197, as said below
- assigned_specialists: int32 [2, 6400, 2], P(None, 'fsdp'), may hold values from 0 to 3, all different within a row
- filling_sequence_place: int32 [2, 8, 800], P(None, 'fsdp'), may hold values from 0 to 799, each once within a row
- leading_scale_factor: bfloat16 [768], P('fsdp'), may hold values from 0.5 to 1.5
- leading_offset_vector: bfloat16 [768], P('fsdp'), may hold values from -1.25 to 1.25
- query_value_matrix: bfloat16 [768, 3, 768], P('fsdp', None, 'tp'), may hold values from -0.21875 to 0.21875
- mixing_projection_matrix: bfloat16 [768, 768], P('tp', 'fsdp'), may hold values from -1.5 to 1.5
- mixing_offset_vector: bfloat16 [768], P('fsdp'), may hold values from -1.25 to 1.25
- central_scale_factor: bfloat16 [768], P('fsdp'), may hold values from 0.5 to 1.5
- central_offset_vector: bfloat16 [768], P('fsdp'), may hold values from -1.25 to 1.25
- gating_projection: bfloat16 [768, 4], P('fsdp'), may hold values from -0.15625 to 0.15625
- specialist_widen_matrix: bfloat16 [4, 768, 3072], P(None, 'fsdp', 'tp'), may hold values from -0.21875 to 0.21875
- specialist_inner_offset: bfloat16 [4, 3072], P(None, 'tp'), may hold values from -0.625 to 0.625
- specialist_contract_matrix: bfloat16 [4, 3072, 768], P(None, 'tp', 'fsdp'), may hold values from -0.4375 to 0.4375
- specialist_final_offset: bfloat16 [4, 768], P(None, 'fsdp'), may hold values from -0.625 to 0.625
Outputs:
- layer_output: float32 [2, 6400, 768], P(None, ('fsdp', 'tp'))
- grad_tokens: float32 [2, 6400, 768], P(None, ('fsdp', 'tp'))
- grad_pregain: float32 [768], P('fsdp')
- grad_preshift: float32 [768], P('fsdp')
- grad_attnweight: float32 [768, 3, 768], P('fsdp', None, 'tp')
- grad_attnoutput: float32 [768, 768], P('tp', 'fsdp')
- grad_attnbias: float32 [768], P('fsdp')
- grad_midgain: float32 [768], P('fsdp')
- grad_midshift: float32 [768], P('fsdp')
- grad_router: float32 [768, 4], P('fsdp')
- grad_hidden: float32 [4, 768, 3072], P(None, 'fsdp', 'tp')
- grad_hiddenbias: float32 [4, 3072], P(None, 'tp')
- grad_expertout: float32 [4, 3072, 768], P(None, 'tp', 'fsdp')
- grad_outputbias: float32 [4, 768], P(None, 'fsdp')
Inputs may be any that keep to these rules, and one draw needn't show every extreme that they name: `picture_valid_count`: the first image of every group in every micro-batch has 197 real tokens.
All inputs are finite; a program needn't handle non-finite values.
Results may differ from a plain program's by a relative error of at most 0.018.
Values may be sent and summed in bfloat16 or wider, within the bound.
A program may use at most 104 MiB of HBM per device.

v0:
```python
import math

import jax
import jax.numpy as jnp
from jax import lax
from jax.sharding import PartitionSpec as P

HEAD_DIM = 64


NORM_EPS = 1e-06
MASK_FILL = -1000000000.0


def norm_parts(values):
    row_mean = jnp.mean(values, axis=-1, keepdims=True)
    centred = values - row_mean
    row_var = jnp.mean(centred * centred, axis=-1, keepdims=True)
    inv_std = lax.rsqrt(row_var + NORM_EPS)
    return (centred * inv_std, inv_std)


def norm_back(grad_out, normed, inv_std, gain_vec):
    scaled = grad_out * gain_vec
    return inv_std * (
        scaled
        - jnp.mean(scaled, axis=-1, keepdims=True)
        - normed * jnp.mean(scaled * normed, axis=-1, keepdims=True)
    )


def gelu_exact(pre_vals):
    return jax.nn.gelu(pre_vals, approximate=False)


def route_slots(route_ids, priority_ids, expert_count, slot_count):
    row_count = route_ids.shape[0]
    order_key = (
        priority_ids[:, None] + row_count * jnp.arange(2, dtype=jnp.int32)[None, :]
    ).reshape(-1)
    chosen = route_ids.reshape(-1)
    rank_order = jnp.argsort(order_key)
    ranked = chosen[rank_order]
    onehot = (ranked[:, None] == jnp.arange(expert_count, dtype=jnp.int32)[None, :]).astype(
        jnp.int32
    )
    before = jnp.cumsum(onehot, axis=0) - onehot
    place_ranked = jnp.sum(before * onehot, axis=1)
    place_all = jnp.zeros_like(place_ranked).at[rank_order].set(place_ranked)
    kept_mask = place_all < slot_count
    slot_ids = jnp.where(kept_mask, chosen * slot_count + place_all, expert_count * slot_count)
    owner_ids = jnp.full((expert_count * slot_count + 1,), 2 * row_count, jnp.int32)
    owner_ids = owner_ids.at[slot_ids].set(jnp.arange(2 * row_count, dtype=jnp.int32))
    return (
        slot_ids.reshape(row_count, 2),
        kept_mask.reshape(row_count, 2),
        owner_ids[: expert_count * slot_count],
    )


def att_scores(queries, keys_all, visible, score_scale):
    scores = (
        jnp.einsum("ishd,ithd->ihst", queries, keys_all, preferred_element_type=jnp.float32)
        * score_scale
    )
    return jnp.where(visible[:, None, None, :], scores, MASK_FILL)


def per_device(
    patch_embeddings,
    upstream_gradient,
    picture_valid_count,
    assigned_specialists,
    filling_sequence_place,
    leading_scale_factor,
    leading_offset_vector,
    query_value_matrix,
    mixing_projection_matrix,
    mixing_offset_vector,
    central_scale_factor,
    central_offset_vector,
    gating_projection,
    specialist_widen_matrix,
    specialist_inner_offset,
    specialist_contract_matrix,
    specialist_final_offset,
):
    micro_count = patch_embeddings.shape[0]
    own_count = patch_embeddings.shape[1]
    model_width = patch_embeddings.shape[2]
    tp_count = lax.axis_size("tp")
    tp_index = lax.axis_index("tp")
    fsdp_index = lax.axis_index("fsdp")
    row_count = own_count * tp_count
    row_start = tp_index * own_count
    image_count = picture_valid_count.shape[1]
    seq_len = row_count // image_count
    expert_count = specialist_widen_matrix.shape[0]
    slot_count = 2 * row_count // expert_count
    head_width = query_value_matrix.shape[2]
    head_count = head_width // HEAD_DIM
    hidden_width = specialist_widen_matrix.shape[2]
    score_scale = 1.0 / math.sqrt(HEAD_DIM)
    expert_iota = jnp.arange(expert_count, dtype=jnp.int32)
    grad_attnw = jnp.zeros((model_width, 3, head_width), jnp.float32)
    grad_attno = jnp.zeros((head_width, model_width), jnp.float32)
    grad_routerw = jnp.zeros((model_width, expert_count), jnp.float32)
    grad_hiddenw = jnp.zeros((expert_count, model_width, hidden_width), jnp.float32)
    grad_expertw = jnp.zeros((expert_count, hidden_width, model_width), jnp.float32)
    grad_outbias = jnp.zeros((expert_count, model_width), jnp.float32)
    grad_hbias = jnp.zeros((expert_count, hidden_width), jnp.float32)
    vector_sums = jnp.zeros((5, model_width), jnp.float32)
    layer_rows = []
    token_grads = []
    hbias_f = specialist_inner_offset.astype(jnp.float32)
    for micro_step in range(micro_count):
        weights_now = (
            lax.all_gather(leading_scale_factor, "fsdp", axis=0, tiled=True),
            lax.all_gather(leading_offset_vector, "fsdp", axis=0, tiled=True),
            lax.all_gather(query_value_matrix, "fsdp", axis=0, tiled=True),
            lax.all_gather(mixing_projection_matrix, "fsdp", axis=1, tiled=True),
            lax.all_gather(mixing_offset_vector, "fsdp", axis=0, tiled=True),
            lax.all_gather(central_scale_factor, "fsdp", axis=0, tiled=True),
            lax.all_gather(central_offset_vector, "fsdp", axis=0, tiled=True),
            lax.all_gather(gating_projection, "fsdp", axis=0, tiled=True),
            lax.all_gather(specialist_widen_matrix, "fsdp", axis=1, tiled=True),
            lax.all_gather(specialist_contract_matrix, "fsdp", axis=2, tiled=True),
            lax.all_gather(specialist_final_offset, "fsdp", axis=1, tiled=True),
        )
        (
            gain_one,
            shift_one,
            qkv_full,
            attno_full,
            attnb_full,
            gain_two,
            shift_two,
            router_full,
            hidden_full,
            expout_full,
            outbias_full,
        ) = weights_now
        token_in = patch_embeddings[micro_step].astype(jnp.float32)
        normed_a, inv_a = norm_parts(token_in)
        initial_standardized_tokens = (
            normed_a * gain_one.astype(jnp.float32) + shift_one.astype(jnp.float32)
        ).astype(jnp.bfloat16)
        rows_in = lax.all_gather(initial_standardized_tokens, "tp", axis=0, tiled=True)
        projected = jnp.einsum(
            "td,dcf->tcf", rows_in, qkv_full, preferred_element_type=jnp.float32
        ).astype(jnp.bfloat16)
        queries = projected[:, 0].reshape(image_count, seq_len, head_count, HEAD_DIM)
        keys_all = projected[:, 1].reshape(image_count, seq_len, head_count, HEAD_DIM)
        values = projected[:, 2].reshape(image_count, seq_len, head_count, HEAD_DIM)
        visible = (
            jnp.arange(seq_len, dtype=jnp.int32)[None, :] < picture_valid_count[micro_step][:, None]
        )
        scores = att_scores(queries, keys_all, visible, score_scale)
        row_top = jnp.max(scores, axis=-1, keepdims=True)
        exp_terms = jnp.exp(scores - row_top)
        row_total = jnp.sum(exp_terms, axis=-1, keepdims=True)
        log_total = row_top + jnp.log(row_total)
        probs_low = (exp_terms / row_total).astype(jnp.bfloat16)
        att_mixed = (
            jnp.einsum("ihst,ithd->ishd", probs_low, values, preferred_element_type=jnp.float32)
            .astype(jnp.bfloat16)
            .reshape(row_count, head_width)
        )
        attn_own = lax.psum_scatter(
            jnp.dot(att_mixed, attno_full, preferred_element_type=jnp.float32),
            "tp",
            scatter_dimension=0,
            tiled=True,
        )
        hidden_one = token_in + attn_own + attnb_full.astype(jnp.float32)
        normed_b, inv_b = norm_parts(hidden_one)
        normed_two = (
            normed_b * gain_two.astype(jnp.float32) + shift_two.astype(jnp.float32)
        ).astype(jnp.bfloat16)
        rows_mid = lax.all_gather(normed_two, "tp", axis=0, tiled=True)
        logits = jnp.dot(rows_mid, router_full, preferred_element_type=jnp.float32)
        logit_top = jnp.max(logits, axis=1, keepdims=True)
        logit_exp = jnp.exp(logits - logit_top)
        router_probs = logit_exp / jnp.sum(logit_exp, axis=1, keepdims=True)
        route_now = assigned_specialists[micro_step]
        pick_hot = (route_now[:, :, None] == expert_iota[None, None, :]).astype(jnp.float32)
        gate_vals = jnp.sum(pick_hot * router_probs[:, None, :], axis=2)
        slot_ids, kept_mask, owner_ids = route_slots(
            route_now, filling_sequence_place[micro_step, 0], expert_count, slot_count
        )
        kept_float = kept_mask.astype(jnp.float32)
        pair_weight = gate_vals * kept_float
        padded_rows = jnp.concatenate([rows_mid, jnp.zeros((1, model_width), jnp.bfloat16)])
        source_rows = jnp.where(owner_ids < 2 * row_count, owner_ids // 2, row_count)
        dispatched = padded_rows[source_rows].reshape(expert_count, slot_count, model_width)
        pre_act = (
            jnp.einsum("ecd,edf->ecf", dispatched, hidden_full, preferred_element_type=jnp.float32)
            + hbias_f[:, None, :]
        )
        act_full, gelu_pull = jax.vjp(gelu_exact, pre_act)
        activation = act_full.astype(jnp.bfloat16)
        expert_part = jnp.einsum(
            "ecf,efd->ecd", activation, expout_full, preferred_element_type=jnp.float32
        )
        expert_pad = jnp.concatenate(
            [
                expert_part.reshape(expert_count * slot_count, model_width),
                jnp.zeros((1, model_width), jnp.float32),
            ]
        )
        picked = expert_pad[slot_ids]
        combined = jnp.sum(pair_weight[:, :, None] * picked, axis=1)
        moe_own = lax.psum_scatter(
            combined.astype(jnp.bfloat16), "tp", scatter_dimension=0, tiled=True
        ).astype(jnp.float32)
        pair_coef = jnp.sum(pair_weight[:, :, None] * pick_hot, axis=1)
        own_coef = lax.dynamic_slice_in_dim(pair_coef, row_start, own_count, 0)
        outbias_f = outbias_full.astype(jnp.float32)
        own_bias = jnp.sum(own_coef[:, :, None] * outbias_f[None, :, :], axis=1)
        layer_rows.append(hidden_one + moe_own + own_bias)
        weights_back = (
            lax.all_gather(leading_scale_factor, "fsdp", axis=0, tiled=True),
            lax.all_gather(leading_offset_vector, "fsdp", axis=0, tiled=True),
            lax.all_gather(query_value_matrix, "fsdp", axis=0, tiled=True),
            lax.all_gather(mixing_projection_matrix, "fsdp", axis=1, tiled=True),
            lax.all_gather(mixing_offset_vector, "fsdp", axis=0, tiled=True),
            lax.all_gather(central_scale_factor, "fsdp", axis=0, tiled=True),
            lax.all_gather(central_offset_vector, "fsdp", axis=0, tiled=True),
            lax.all_gather(gating_projection, "fsdp", axis=0, tiled=True),
            lax.all_gather(specialist_widen_matrix, "fsdp", axis=1, tiled=True),
            lax.all_gather(specialist_contract_matrix, "fsdp", axis=2, tiled=True),
            lax.all_gather(specialist_final_offset, "fsdp", axis=1, tiled=True),
        )
        (
            gain_one,
            shift_one,
            qkv_full,
            attno_full,
            attnb_full,
            gain_two,
            shift_two,
            router_full,
            hidden_full,
            expout_full,
            outbias_full,
        ) = weights_back
        cot_own = upstream_gradient[micro_step]
        cot_full = lax.all_gather(cot_own, "tp", axis=0, tiled=True)
        cot_f = cot_full.astype(jnp.float32)
        gate_part = jnp.sum(picked * cot_f[:, None, :], axis=2)
        gate_total = lax.psum(gate_part, "tp")
        bias_dot = jnp.einsum(
            "rd,ed->re", cot_full, outbias_full, preferred_element_type=jnp.float32
        )
        d_gate = (gate_total + jnp.sum(pick_hot * bias_dot[:, None, :], axis=2)) * kept_float
        scaled_rows = (pair_weight[:, :, None] * cot_f[:, None, :]).reshape(
            2 * row_count, model_width
        )
        scaled_pad = jnp.concatenate([scaled_rows, jnp.zeros((1, model_width), jnp.float32)])
        d_slot = scaled_pad[owner_ids].reshape(expert_count, slot_count, model_width)
        grad_outbias = grad_outbias + jnp.sum(d_slot, axis=1)
        slot_low = d_slot.astype(jnp.bfloat16)
        grad_expertw = grad_expertw + jnp.einsum(
            "ecf,ecd->efd", activation, slot_low, preferred_element_type=jnp.float32
        )
        d_act = jnp.einsum(
            "ecd,efd->ecf", slot_low, expout_full, preferred_element_type=jnp.float32
        )
        d_pre = gelu_pull(d_act)[0].astype(jnp.bfloat16)
        grad_hbias = grad_hbias + jnp.sum(d_pre.astype(jnp.float32), axis=1)
        grad_hiddenw = grad_hiddenw + jnp.einsum(
            "ecd,ecf->edf", dispatched, d_pre, preferred_element_type=jnp.float32
        )
        d_disp = jnp.einsum("ecf,edf->ecd", d_pre, hidden_full, preferred_element_type=jnp.float32)
        disp_pad = jnp.concatenate(
            [
                d_disp.reshape(expert_count * slot_count, model_width),
                jnp.zeros((1, model_width), jnp.float32),
            ]
        )
        mid_part = jnp.sum(disp_pad[slot_ids], axis=1)
        d_prob = jnp.sum(d_gate[:, :, None] * pick_hot, axis=1)
        d_logits = (
            router_probs * (d_prob - jnp.sum(router_probs * d_prob, axis=1, keepdims=True))
        ).astype(jnp.bfloat16)
        grad_routerw = grad_routerw + jnp.einsum(
            "rd,re->de", rows_mid, d_logits, preferred_element_type=jnp.float32
        )
        own_logits = lax.dynamic_slice_in_dim(d_logits, row_start, own_count, 0)
        router_back = jnp.einsum(
            "re,de->rd", own_logits, router_full, preferred_element_type=jnp.float32
        )
        mid_own = lax.psum_scatter(mid_part, "tp", scatter_dimension=0, tiled=True) + router_back
        d_hidden = cot_own.astype(jnp.float32) + norm_back(
            mid_own, normed_b, inv_b, gain_two.astype(jnp.float32)
        )
        hidden_low = d_hidden.astype(jnp.bfloat16)
        hidden_full_rows = lax.all_gather(hidden_low, "tp", axis=0, tiled=True)
        grad_attno = grad_attno + jnp.einsum(
            "tf,te->fe", att_mixed, hidden_full_rows, preferred_element_type=jnp.float32
        )
        d_mixed = jnp.einsum(
            "te,fe->tf", hidden_full_rows, attno_full, preferred_element_type=jnp.float32
        ).astype(jnp.bfloat16)
        d_mixed = d_mixed.reshape(image_count, seq_len, head_count, HEAD_DIM)
        scores = att_scores(queries, keys_all, visible, score_scale)
        att_probs = jnp.exp(scores - log_total)
        d_prob_att = jnp.einsum(
            "ishd,ithd->ihst", d_mixed, values, preferred_element_type=jnp.float32
        )
        d_scores = (
            att_probs * (d_prob_att - jnp.sum(att_probs * d_prob_att, axis=-1, keepdims=True))
        ).astype(jnp.bfloat16)
        d_queries = (
            jnp.einsum("ihst,ithd->ishd", d_scores, keys_all, preferred_element_type=jnp.float32)
            * score_scale
        ).astype(jnp.bfloat16)
        d_keys = (
            jnp.einsum("ihst,ishd->ithd", d_scores, queries, preferred_element_type=jnp.float32)
            * score_scale
        ).astype(jnp.bfloat16)
        d_values = jnp.einsum(
            "ihst,ishd->ithd", probs_low, d_mixed, preferred_element_type=jnp.float32
        ).astype(jnp.bfloat16)
        d_projected = jnp.stack(
            [
                d_queries.reshape(row_count, head_width),
                d_keys.reshape(row_count, head_width),
                d_values.reshape(row_count, head_width),
            ],
            axis=1,
        )
        grad_attnw = grad_attnw + jnp.einsum(
            "td,tcf->dcf", rows_in, d_projected, preferred_element_type=jnp.float32
        )
        low_own = lax.psum_scatter(
            jnp.einsum(
                "tcf,dcf->td", d_projected, qkv_full, preferred_element_type=jnp.float32
            ).astype(jnp.bfloat16),
            "tp",
            scatter_dimension=0,
            tiled=True,
        ).astype(jnp.float32)
        token_grads.append(
            d_hidden + norm_back(low_own, normed_a, inv_a, gain_one.astype(jnp.float32))
        )
        vector_sums = vector_sums + jnp.stack(
            [
                jnp.sum(low_own * normed_a, axis=0),
                jnp.sum(low_own, axis=0),
                jnp.sum(d_hidden, axis=0),
                jnp.sum(mid_own * normed_b, axis=0),
                jnp.sum(mid_own, axis=0),
            ]
        )
    reduced = (
        lax.psum_scatter(
            grad_attnw.astype(jnp.bfloat16), "fsdp", scatter_dimension=0, tiled=True
        ).astype(jnp.float32),
        lax.psum_scatter(
            grad_attno.astype(jnp.bfloat16), "fsdp", scatter_dimension=1, tiled=True
        ).astype(jnp.float32),
        lax.psum_scatter(
            grad_routerw.astype(jnp.bfloat16), "fsdp", scatter_dimension=0, tiled=True
        ).astype(jnp.float32),
        lax.psum_scatter(
            grad_hiddenw.astype(jnp.bfloat16), "fsdp", scatter_dimension=1, tiled=True
        ).astype(jnp.float32),
        lax.psum_scatter(
            grad_expertw.astype(jnp.bfloat16), "fsdp", scatter_dimension=2, tiled=True
        ).astype(jnp.float32),
        lax.psum_scatter(
            grad_outbias.astype(jnp.bfloat16), "fsdp", scatter_dimension=1, tiled=True
        ).astype(jnp.float32),
    )
    bias_place = jnp.zeros((expert_count, hidden_width * tp_count), jnp.float32)
    bias_place = lax.dynamic_update_slice_in_dim(bias_place, grad_hbias, tp_index * hidden_width, 1)
    bias_total, vector_total = lax.psum((bias_place, vector_sums), ("fsdp", "tp"))
    own_width = leading_scale_factor.shape[0]
    own_vectors = lax.dynamic_slice_in_dim(vector_total, fsdp_index * own_width, own_width, 1)
    own_hbias = lax.dynamic_slice_in_dim(bias_total, tp_index * hidden_width, hidden_width, 1)
    return (
        jnp.stack(layer_rows),
        jnp.stack(token_grads),
        own_vectors[0],
        own_vectors[1],
        reduced[0],
        reduced[1],
        own_vectors[2],
        own_vectors[3],
        own_vectors[4],
        reduced[2],
        reduced[3],
        own_hbias,
        reduced[4],
        reduced[5],
    )


def solution(mesh):
    placed = (
        P(None, ("fsdp", "tp"), None),
        P(None, ("fsdp", "tp"), None),
        P(None, "fsdp"),
        P(None, "fsdp", None),
        P(None, "fsdp", None),
        P("fsdp"),
        P("fsdp"),
        P("fsdp", None, "tp"),
        P("tp", "fsdp"),
        P("fsdp"),
        P("fsdp"),
        P("fsdp"),
        P("fsdp", None),
        P(None, "fsdp", "tp"),
        P(None, "tp"),
        P(None, "tp", "fsdp"),
        P(None, "fsdp"),
    )
    return jax.shard_map(
        per_device,
        mesh=mesh,
        in_specs=placed,
        out_specs=(
            P(None, ("fsdp", "tp"), None),
            P(None, ("fsdp", "tp"), None),
            P("fsdp"),
            P("fsdp"),
            P("fsdp", None, "tp"),
            P("tp", "fsdp"),
            P("fsdp"),
            P("fsdp"),
            P("fsdp"),
            P("fsdp", None),
            P(None, "fsdp", "tp"),
            P(None, "tp"),
            P(None, "tp", "fsdp"),
            P(None, "fsdp"),
        ),
        check_vma=False,
    )
```

profile of v0, /device:TPU:0, one launch (start us, length us, event | category | flops | bytes accessed | tf_op | source)
XLA Modules:
  0.0 1245.3 jit_solution(11719639486313956075)
XLA Ops:
  16.0 38.8 %all-reduce.17 = (bf16[768]{0:T(1024)(128)(2,1)S(1)}, bf16[768]{0:T(1024)(128)(2,1)S(1)}, bf16[768]{0:T(1024)(128)(2,1)S(1)}, bf16[768]{0:T(1024)(128)(2,1)S(1)}, bf16[768]{0:T(1024)(128)(2,1)S(1)}) all-reduce(bf16[768]{0:T(1024)(128)(2,1)S(1)} %dynamic-update-slice.1, ...), channel_id=1, replica_groups=mesh['fsdp'=8,'tp'=4] {'fsdp'}, use_global_device_ids=true, to_apply=%add.11 | all-reduce | flops 3840 | bytes 15360
  59.5 36.6 %all_gather.41 = bf16[768,3,192]{2,1,0:T(4,128)(2,1)S(1)} all-gather(bf16[96,3,192]{2,1,0:T(4,128)(2,1)S(1)} %copy.207), channel_id=1, replica_groups=mesh['fsdp'=8,'tp'=4] {'fsdp'}, dimensions={0}, use_global_device_ids=true | all-gather | bytes 995328 | tf_op jit(solution)/shard_map/all_gather | solution.py:120
  97.1 31.0 %all_gather.42 = bf16[192,768]{0,1:T(8,128)(2,1)S(1)} all-gather(bf16[192,96]{0,1:T(8,128)(2,1)S(1)} %copy.214), channel_id=1, replica_groups=mesh['fsdp'=8,'tp'=4] {'fsdp'}, dimensions={1}, use_global_device_ids=true | all-gather | bytes 331776 | tf_op jit(solution)/shard_map/all_gather | solution.py:121
  151.3 19.4 %reduce-scatter.25.cloned.1.call-done = f32[200,768]{1,0:T(8,128)} async-done(((f32[800,768]{1,0:T(8,128)}), f32[200,768]{1,0:T(8,128)}) %reduce-scatter.25.cloned.1.call-update) | async-done | bytes 614416 | tf_op jit(solution)/shard_map/reduce_scatter | solution.py:169
  170.7 36.3 %reduce-scatter.21.cloned.1.call-done = f32[200,768]{1,0:T(8,128)} async-done(((f32[800,768]{1,0:T(8,128)}), f32[200,768]{1,0:T(8,128)}) %reduce-scatter.21.cloned.1.call-update) | async-done | bytes 614416 | tf_op jit(solution)/shard_map/reduce_scatter | solution.py:169
  212.7 20.5 %all-gather.3 = bf16[8,96,4]{1,2,0:T(4,128)(2,1)S(1)} all-gather(bf16[1,96,4]{1,2,0:T(4,128)(2,1)S(1)} %bitcast.318), channel_id=1, replica_groups=mesh['fsdp'=8,'tp'=4] {'fsdp'}, dimensions={0}, use_global_device_ids=true | all-gather | bytes 6912 | tf_op jit(solution)/shard_map/all_gather | solution.py:128
  233.3 16.3 %all-gather.2 = bf16[8,96,4]{1,2,0:T(4,128)(2,1)S(1)} all-gather(bf16[1,96,4]{1,2,0:T(4,128)(2,1)S(1)} %bitcast.319), channel_id=1, replica_groups=mesh['fsdp'=8,'tp'=4] {'fsdp'}, dimensions={0}, use_global_device_ids=true | all-gather | bytes 6912 | tf_op jit(solution)/shard_map/all_gather | solution.py:125
  261.0 8.8 gather_fusion.3
  271.6 8.8 scatter_custom_fusion.2
  280.8 8.8 gather_fusion
  291.4 9.3 scatter_custom_fusion
  306.2 7.2 mul.529
  319.9 8.8 scatter_custom_fusion.3
  331.7 9.0 scatter_custom_fusion.1
  340.9 6.3 gather_fusion.4
  347.2 6.3 gather_fusion.1
  358.9 10.1 gather_fusion.6
  382.0 24.3 %multiply_convert_fusion = (bf16[4,400,768]{2,1,0:T(8,128)(2,1)S(1)}, f32[4,400,768]{2,1,0:T(8,128)}, bf16[4,400,768]{2,1,0:T(8,128)(2,1)}, f32[4,400,768]{2,1,0:T(8,128)}) fusion(f32[4,400,768]{2,1,0:T(8,128)S(1)} %fusion.153, f32[4,768]{1,0:T(4,128)S(1)} %convert_element_type.261, u8[400,768]{1,0:T(8,128)(4,1)S(1)} %get-tuple-element.48, ...), kind=kLoop, calls=%fused_computation.36 | loop fusion | flops 173260800 | bytes 25817088 | tf_op jit(solution)/shard_map/convert_element_type | solution.py:201
  406.3 42.9 %all-gather.21.cloned.1.call-done = bf16[4,768,768]{1,2,0:T(8,128)(2,1)} async-done(((bf16[4,768,96]{1,2,0:T(8,128)(2,1)}), bf16[4,768,768]{1,2,0:T(8,128)(2,1)}) %all-gather.21.cloned.1.call-update) | async-done | bytes 4718608 | tf_op jit(solution)/shard_map/all_gather | solution.py:127
  449.2 10.8 convert_reduce_fusion.1
  465.3 9.9 gather_fusion.7
  475.2 7.2 reshape.447
  482.4 9.7 reduce_sum.531
  500.9 7.6 mul.562
  514.5 9.9 gather_fusion.8
  524.4 10.6 convert_reduce_fusion
  542.9 9.9 gather_fusion.9
  552.8 7.1 reshape.463
  559.9 9.7 reduce_sum.542
  578.6 10.1 gather_fusion.2
  588.7 7.0 reshape.403
  595.9 11.6 multiply_reduce_fusion.1
  614.8 10.0 gather_fusion.5
  624.7 7.2 reshape.427
  632.5 11.4 multiply_reduce_fusion
  644.1 10.3 all-reduce.16
  662.8 17.2 %reduce-scatter.27.cloned.1.call-done = bf16[200,768]{1,0:T(8,128)(2,1)} async-done(((bf16[800,768]{1,0:T(8,128)(2,1)}), bf16[200,768]{1,0:T(8,128)(2,1)}) %reduce-scatter.27.cloned.1.call-update) | async-done | bytes 307216 | tf_op jit(solution)/shard_map/reduce_scatter | solution.py:213
  695.8 6.3 all-gather.27.cloned.1.call-done
  713.0 8.4 all-gather.29.cloned.1.call-done
  788.3 7.2 add_convert_fusion
  797.2 52.1 %reduce-scatter.47.cloned.1.call-done = bf16[96,4]{1,0:T(8,128)(2,1)} async-done(((bf16[768,4]{1,0:T(8,128)(2,1)}), bf16[96,4]{1,0:T(8,128)(2,1)}) %reduce-scatter.47.cloned.1.call-update) | async-done | bytes 784
  852.1 61.0 %reduce-scatter.43.cloned.1.call-done = bf16[96,192]{1,0:T(8,128)(2,1)} async-done(((bf16[768,192]{1,0:T(8,128)(2,1)}), bf16[96,192]{1,0:T(8,128)(2,1)}) %reduce-scatter.43.cloned.1.call-update) | async-done | bytes 36880
  914.6 65.3 %reduce-scatter.37.cloned.1.call-done = bf16[96,3,192]{2,0,1:T(8,128)(2,1)} async-done(((bf16[768,3,192]{2,0,1:T(8,128)(2,1)}), bf16[96,3,192]{2,0,1:T(8,128)(2,1)}) %reduce-scatter.37.cloned.1.call-update) | async-done | bytes 110608 | tf_op jit(solution)/shard_map/reduce_scatter | solution.py:357
  981.6 26.6 %reduce-scatter.31.cloned.1.call-done = bf16[200,768]{1,0:T(8,128)(2,1)} async-done(((bf16[800,768]{1,0:T(8,128)(2,1)}), bf16[200,768]{1,0:T(8,128)(2,1)}) %reduce-scatter.31.cloned.1.call-update) | async-done | bytes 307216 | tf_op jit(solution)/shard_map/reduce_scatter | solution.py:336
  1008.2 28.8 %reduce-scatter.35.cloned.1.call-done = bf16[200,768]{1,0:T(8,128)(2,1)} async-done(((bf16[800,768]{1,0:T(8,128)(2,1)}), bf16[200,768]{1,0:T(8,128)(2,1)}) %reduce-scatter.35.cloned.1.call-update) | async-done | bytes 307216 | tf_op jit(solution)/shard_map/reduce_scatter | solution.py:336
  1038.9 42.5 %all-reduce.15 = (f32[5,768]{1,0:T(8,128)S(1)}, f32[4,3072]{1,0:T(4,128)S(1)}) all-reduce(f32[5,768]{1,0:T(8,128)S(1)} %add.383, f32[4,3072]{1,0:T(4,128)S(1)} %add_dynamic-update-slice_fusion), channel_id=1, replica_groups=mesh['fsdp'=8,'tp'=4] {'fsdp','tp'}, use_global_device_ids=true, to_apply=%region_76.77 | all-reduce | flops 16128 | bytes 129024 | tf_op jit(solution)/shard_map/psum | solution.py:378
  1085.3 52.0 %reduce-scatter.39.cloned.1.call-done = bf16[4,96,768]{2,1,0:T(8,128)(2,1)} async-done(((bf16[4,768,768]{2,1,0:T(8,128)(2,1)}), bf16[4,96,768]{2,1,0:T(8,128)(2,1)}) %reduce-scatter.39.cloned.1.call-update) | async-done | bytes 589840 | tf_op jit(solution)/shard_map/reduce_scatter | solution.py:366
  1139.5 96.5 %reduce-scatter.41.cloned.1.call-done = bf16[4,768,96]{1,2,0:T(8,128)(2,1)} async-done(((bf16[4,768,768]{1,2,0:T(8,128)(2,1)}), bf16[4,768,96]{1,2,0:T(8,128)(2,1)}) %reduce-scatter.41.cloned.1.call-update) | async-done | bytes 589840 | tf_op jit(solution)/shard_map/reduce_scatter | solution.py:369
  (586 shorter events, 254.2 us)
Async XLA Ops:
  7.2 89.8 %copy-start.123 = (s32[2,4]{1,0:T(2,128)S(1)}, s32[2,4]{1,0:T(2,128)}, u32[]{:S(2)}) copy-start(s32[2,4]{1,0:T(2,128)} %param.19) | copy-start | bytes 100
  7.2 89.8 %copy-start.94 = (bf16[192,96]{1,0:T(8,128)(2,1)S(1)}, bf16[192,96]{1,0:T(8,128)(2,1)}, u32[]{:S(2)}) copy-start(bf16[192,96]{1,0:T(8,128)(2,1)} %param.25) | copy-start | bytes 110596
  7.2 120.9 %all-gather.23.cloned.1.call-start = ((), (), s32[]{:S(2)}) async-start(), calls=%async_computation.20 | async-start | bytes 1536000 | tf_op jit(solution)/shard_map/all_gather | solution.py:148
  57.6 81.1 %all-gather.15.cloned.1.call-start = ((), (), s32[]{:S(2)}) async-start(), calls=%async_computation.14 | async-start | bytes 1536000 | tf_op jit(solution)/shard_map/all_gather | solution.py:148
  58.4 112.4 %reduce-scatter.25.cloned.1.call-start = ((), (), s32[]{:S(2)}) async-start(), calls=%async_computation.21 | async-start | bytes 3072000 | tf_op jit(solution)/shard_map/reduce_scatter | solution.py:169
  138.6 68.4 %reduce-scatter.21.cloned.1.call-start = ((), (), s32[]{:S(2)}) async-start(), calls=%async_computation.15 | async-start | bytes 3072000 | tf_op jit(solution)/shard_map/reduce_scatter | solution.py:169
  146.7 60.4 %copy-start.12 = (bf16[2,200,768]{2,1,0:T(8,128)(2,1)S(1)}, bf16[2,200,768]{2,1,0:T(8,128)(2,1)}, u32[]{:S(2)}) copy-start(bf16[2,200,768]{2,1,0:T(8,128)(2,1)} %param.17) | copy-start | bytes 1843204
  147.3 61.2 %copy-start.41 = (bf16[800,192]{0,1:T(8,128)(2,1)}, bf16[800,192]{0,1:T(8,128)(2,1)S(1)}, u32[]{:S(2)}) copy-start(bf16[800,192]{0,1:T(8,128)(2,1)S(1)} %reshape.364) | copy-start | bytes 921604
  149.3 63.3 %copy-start.121 = (bf16[4,96]{1,0:T(4,128)(2,1)S(1)}, bf16[4,96]{1,0:T(4,128)(2,1)}, u32[]{:S(2)}) copy-start(bf16[4,96]{1,0:T(4,128)(2,1)} %param.33) | copy-start | bytes 2308
  149.3 83.9 %copy-start.116 = (s32[2,800,2]{1,2,0:T(2,128)S(1)}, s32[2,800,2]{1,2,0:T(2,128)}, u32[]{:S(2)}) copy-start(s32[2,800,2]{1,2,0:T(2,128)} %param.20) | copy-start | bytes 38404
  149.4 83.9 %copy-start.122 = (bf16[96,4]{0,1:T(4,128)(2,1)S(1)}, bf16[96,4]{0,1:T(4,128)(2,1)}, u32[]{:S(2)}) copy-start(bf16[96,4]{0,1:T(4,128)(2,1)} %param.29) | copy-start | bytes 2308
  149.4 100.3 %copy-start.119 = (s32[2,1,800]{2,1,0:T(1,128)S(1)}, s32[2,1,800]{2,1,0:T(1,128)}, u32[]{:S(2)}) copy-start(s32[2,1,800]{2,1,0:T(1,128)} %param.21) | copy-start | bytes 19204
  149.4 151.4 %all-gather.31.cloned.1.call-start = ((), (), s32[]{:S(2)}) async-start(), calls=%async_computation.33 | async-start | bytes 1536000 | tf_op jit(solution)/shard_map/all_gather | solution.py:248
  150.3 164.7 %all-gather.33.cloned.1.call-start = ((), (), s32[]{:S(2)}) async-start(), calls=%async_computation.34 | async-start | bytes 1536000 | tf_op jit(solution)/shard_map/all_gather | solution.py:248
  150.9 165.9 %all-gather.25.cloned.1.call-start = ((), (), s32[]{:S(2)}) async-start(), calls=%async_computation.22 | async-start | bytes 1536000 | tf_op jit(solution)/shard_map/all_gather | solution.py:180
  151.3 98.4 %copy-start.84 = (f32[768]{0:T(1024)}, f32[768]{0:T(1024)S(1)}, u32[]{:S(2)}) copy-start(f32[768]{0:T(1024)S(1)} %convert_element_type.258) | copy-start | bytes 9220
  210.5 118.2 %all-gather.17.cloned.1.call-start = ((), (), s32[]{:S(2)}) async-start(), calls=%async_computation.16 | async-start | bytes 1536000 | tf_op jit(solution)/shard_map/all_gather | solution.py:180
  211.3 157.8 %all-gather.19.cloned.1.call-start = ((), (), s32[]{:S(2)}) async-start(), calls=%async_computation.17 | async-start | bytes 5308416 | tf_op jit(solution)/shard_map/all_gather | solution.py:126
  212.0 237.2 %all-gather.21.cloned.1.call-start = ((), (), s32[]{:S(2)}) async-start(), calls=%async_computation.18 | async-start | bytes 5308416 | tf_op jit(solution)/shard_map/all_gather | solution.py:127
  212.6 444.0 %reduce-scatter.29.cloned.1.call-start = ((), (), s32[]{:S(2)}) async-start(), calls=%async_computation.24 | async-start | bytes 3072000 | tf_op jit(solution)/shard_map/reduce_scatter | solution.py:293
  233.3 85.5 %copy-start.86 = (s32[800,2]{0,1:T(2,128)}, s32[800,2]{0,1:T(2,128)S(1)}, u32[]{:S(2)}) copy-start(s32[800,2]{0,1:T(2,128)S(1)} %get-tuple-element.111) | copy-start | bytes 19204
  233.3 97.3 %copy-start.88 = (s32[800,2]{0,1:T(2,128)}, s32[800,2]{0,1:T(2,128)S(1)}, u32[]{:S(2)}) copy-start(s32[800,2]{0,1:T(2,128)S(1)} %get-tuple-element.110) | copy-start | bytes 19204
  249.7 79.1 %copy-start.63 = (bf16[768,4]{0,1:T(4,128)(2,1)}, bf16[768,4]{0,1:T(4,128)(2,1)S(1)}, u32[]{:S(2)}) copy-start(bf16[768,4]{0,1:T(4,128)(2,1)S(1)} %reshape.532) | copy-start | bytes 18436
  382.0 77.9 %slice-start = ((s8[4718592]{0:T(1024)(128)(4,1)}), s8[524288]{0:T(1024)(128)(4,1)S(1)}, s32[]{:S(2)}) async-start(s8[4718592]{0:T(1024)(128)(4,1)} %bitcast.290), calls=%async_computation.38 | async-start | bytes 1048576
  406.3 201.5 %copy-start.5 = (bf16[4,400,768]{2,1,0:T(8,128)(2,1)}, bf16[4,400,768]{2,1,0:T(8,128)(2,1)S(1)}, u32[]{:S(2)}) copy-start(bf16[4,400,768]{2,1,0:T(8,128)(2,1)S(1)} %get-tuple-element.79) | copy-start | bytes 7372804
  492.1 166.0 %reduce-scatter.33.cloned.1.call-start = ((), (), s32[]{:S(2)}) async-start(), calls=%async_computation.27 | async-start | bytes 3072000 | tf_op jit(solution)/shard_map/reduce_scatter | solution.py:293
  569.6 89.9 %reduce-scatter.23.cloned.1.call-start = ((), (), s32[]{:S(2)}) async-start(), calls=%async_computation.19 | async-start | bytes 1536000 | tf_op jit(solution)/shard_map/reduce_scatter | solution.py:213
  607.8 72.2 %reduce-scatter.27.cloned.1.call-start = ((), (), s32[]{:S(2)}) async-start(), calls=%async_computation.23 | async-start | bytes 1536000 | tf_op jit(solution)/shard_map/reduce_scatter | solution.py:213
  654.7 47.5 %all-gather.27.cloned.1.call-start = ((), (), s32[]{:S(2)}) async-start(), calls=%async_computation.25 | async-start | bytes 1536000 | tf_op jit(solution)/shard_map/all_gather | solution.py:298
  684.3 37.1 %all-gather.29.cloned.1.call-start = ((), (), s32[]{:S(2)}) async-start(), calls=%async_computation.28 | async-start | bytes 1536000 | tf_op jit(solution)/shard_map/all_gather | solution.py:298
  685.1 110.6 %reduce-scatter.45.cloned.1.call-start = ((), (), s32[]{:S(2)}) async-start(), calls=%async_computation.36 | async-start | bytes 221184
  694.8 154.5 %reduce-scatter.47.cloned.1.call-start = ((), (), s32[]{:S(2)}) async-start(), calls=%async_computation.37 | async-start | bytes 221184
  695.8 217.3 %reduce-scatter.43.cloned.1.call-start = ((), (), s32[]{:S(2)}) async-start(), calls=%async_computation.35 | async-start | bytes 442368
  756.7 223.3 %reduce-scatter.37.cloned.1.call-start = ((), (), s32[]{:S(2)}) async-start(), calls=%async_computation.30 | async-start | bytes 1327104 | tf_op jit(solution)/shard_map/reduce_scatter | solution.py:357
  766.7 241.5 %reduce-scatter.31.cloned.1.call-start = ((), (), s32[]{:S(2)}) async-start(), calls=%async_computation.26 | async-start | bytes 1536000 | tf_op jit(solution)/shard_map/reduce_scatter | solution.py:336
  770.2 266.8 %reduce-scatter.35.cloned.1.call-start = ((), (), s32[]{:S(2)}) async-start(), calls=%async_computation.29 | async-start | bytes 1536000 | tf_op jit(solution)/shard_map/reduce_scatter | solution.py:336
  772.5 364.9 %reduce-scatter.39.cloned.1.call-start = ((), (), s32[]{:S(2)}) async-start(), calls=%async_computation.31 | async-start | bytes 5308416 | tf_op jit(solution)/shard_map/reduce_scatter | solution.py:366
  782.4 453.6 %reduce-scatter.41.cloned.1.call-start = ((), (), s32[]{:S(2)}) async-start(), calls=%async_computation.32 | async-start | bytes 5308416 | tf_op jit(solution)/shard_map/reduce_scatter | solution.py:369
  788.2 62.5 %copy-start.111 = (f32[768]{0:T(1024)S(1)}, f32[768]{0:T(1024)}, u32[]{:S(2)}) copy-start(f32[768]{0:T(1024)} %get-tuple-element.73) | copy-start | bytes 9220
  788.3 62.5 %copy-start.109 = (f32[768]{0:T(1024)S(1)}, f32[768]{0:T(1024)}, u32[]{:S(2)}) copy-start(f32[768]{0:T(1024)} %get-tuple-element.28) | copy-start | bytes 9220
  795.5 55.4 %copy-start.44 = (f32[1,200,768]{2,1,0:T(8,128)S(1)}, f32[1,200,768]{2,1,0:T(8,128)}, u32[]{:S(2)}) copy-start(f32[1,200,768]{2,1,0:T(8,128)} %get-tuple-element.105) | copy-start | bytes 1843204
  795.5 241.5 %copy-start.13 = (bf16[2,200,768]{2,1,0:T(8,128)(2,1)S(1)}, bf16[2,200,768]{2,1,0:T(8,128)(2,1)}, u32[]{:S(2)}) copy-start(bf16[2,200,768]{2,1,0:T(8,128)(2,1)} %param.17) | copy-start | bytes 1843204
  795.5 241.5 %copy-start.83 = (f32[768]{0:T(1024)S(1)}, f32[768]{0:T(1024)}, u32[]{:S(2)}) copy-start(f32[768]{0:T(1024)} %copy-done.82) | copy-start | bytes 9220
  795.5 241.5 %copy-start.98 = (f32[200]{0:T(256)S(1)}, f32[200]{0:T(256)}, u32[]{:S(2)}) copy-start(f32[200]{0:T(256)} %copy-done.97) | copy-start | bytes 2404
  795.5 241.5 %copy-start.100 = (f32[200]{0:T(256)S(1)}, f32[200]{0:T(256)}, u32[]{:S(2)}) copy-start(f32[200]{0:T(256)} %copy-done.99) | copy-start | bytes 2404
  795.5 241.5 %copy-start.106 = (f32[200]{0:T(256)S(1)}, f32[200]{0:T(256)}, u32[]{:S(2)}) copy-start(f32[200]{0:T(256)} %copy-done.105) | copy-start | bytes 2404
  795.5 241.5 %copy-start.108 = (f32[200]{0:T(256)S(1)}, f32[200]{0:T(256)}, u32[]{:S(2)}) copy-start(f32[200]{0:T(256)} %copy-done.107) | copy-start | bytes 2404
  795.6 286.5 %copy-start.31 = (f32[200,768]{1,0:T(8,128)S(1)}, f32[200,768]{1,0:T(8,128)}, u32[]{:S(2)}) copy-start(f32[200,768]{1,0:T(8,128)} %copy-done.30) | copy-start | bytes 1843204
  (102 other events, 1279.0 us)
Sparse Core Ops, SparseCore 0:
  57.7 15.0 all-gather.22
  74.9 17.7 all-gather.14
  138.8 31.9 reduce-scatter.24
  173.3 33.6 reduce-scatter.20
  208.4 17.7 all-gather.30
  228.2 17.7 all-gather.32
  248.1 18.8 all-gather.24
  269.2 17.7 all-gather.16
  289.2 79.8 all-gather.18
  371.1 78.0 all-gather.20
  492.2 31.7 reduce-scatter.28
  569.7 32.1 reduce-scatter.32
  607.9 24.7 reduce-scatter.22
  654.8 25.0 reduce-scatter.26
  684.4 17.7 all-gather.26
  703.6 17.7 all-gather.28
  725.0 61.0 reduce-scatter.44
  789.3 60.0 reduce-scatter.46
  852.6 60.3 reduce-scatter.42
  916.9 63.0 reduce-scatter.36
  983.1 25.0 reduce-scatter.30
  1010.9 26.0 reduce-scatter.34
  1040.6 96.6 reduce-scatter.38
  1140.9 95.1 reduce-scatter.40
where the time goes:
time: 1260 us; the launch traced here: 1250 us
  waiting for transfers between devices  517 us (41%)
  local copies, waits for them, and re-layouts  253 us (20%)
  blocking collectives  196 us (16%)
  other arithmetic  131 us (10%)
  matrix products  129 us (10%)
  between operations  17.8 us (1%)
    unnamed x27, waiting for transfers between devices  117 us
    reduce_scatter x1, waiting for transfers between devices, per_device(): lax.psum_scatter(grad_expertw.astype(jnp.bfloat16), 'fsdp', scatter_dimen...  96.5 us
    reduce_scatter x1, waiting for transfers between devices, per_device(): lax.psum_scatter(grad_attnw.astype(jnp.bfloat16), 'fsdp', scatter_dimensi...  65.3 us
    reduce_scatter x2, waiting for transfers between devices, per_device(): lax.psum_scatter(jnp.dot(att_mixed, attno_full, preferred_element_type=jn...  55.8 us
    reduce_scatter x2, waiting for transfers between devices, per_device(): lax.psum_scatter(jnp.einsum('tcf,dcf->td', d_projected, qkv_full, preferr...  55.4 us
    reduce_scatter x1, waiting for transfers between devices, per_device(): lax.psum_scatter(grad_hiddenw.astype(jnp.bfloat16), 'fsdp', scatter_dimen...  52 us
    all_gather x1, waiting for transfers between devices, per_device(): lax.all_gather(specialist_contract_matrix, 'fsdp', axis=2, tiled=True)  42.9 us
    psum x1, blocking collectives, per_device(): lax.psum((bias_place, vector_sums), ('fsdp', 'tp'))  42.5 us
  transfers between devices with their start and end apart: 24, of which 14 were waited for; matrix products, arithmetic and copies ran while one was open for 36% of the time, Pallas kernels for 0%

commit v1 on v0

v1 whole, which is shorter than its diff:
```python
import functools
import math

import jax
import jax.numpy as jnp
from jax import lax
from jax.experimental import pallas as pl
from jax.experimental.pallas import tpu as pltpu
from jax.sharding import PartitionSpec as P

HEAD_DIM = 64
NORM_EPS = 1e-06
MASK_FILL = -1000000000.0
MESH = pl.DeviceIdType.MESH
BF = jnp.bfloat16
F32 = jnp.float32
DMA = pltpu.SemaphoreType.DMA

EARLY_GATHER = 2
EARLY_REDUCE = 2
VMEM_LIMIT = 60 << 20


def dot_nn(a, b):
    return lax.dot_general(a, b, (((1,), (0,)), ((), ())), preferred_element_type=F32)


def dot_nt(a, b):
    return lax.dot_general(a, b, (((1,), (1,)), ((), ())), preferred_element_type=F32)


def dot_tn(a, b):
    return lax.dot_general(a, b, (((0,), (0,)), ((), ())), preferred_element_type=F32)


def norm_parts(values):
    row_mean = jnp.mean(values, axis=-1, keepdims=True)
    centred = values - row_mean
    row_var = jnp.mean(centred * centred, axis=-1, keepdims=True)
    inv_std = lax.rsqrt(row_var + NORM_EPS)
    return centred * inv_std, inv_std


def norm_back(scaled, normed, inv_std):
    return inv_std * (
        scaled
        - jnp.mean(scaled, axis=-1, keepdims=True)
        - normed * jnp.mean(scaled * normed, axis=-1, keepdims=True)
    )


def gelu_parts(x):
    z = jnp.abs(x) * (1.0 / math.sqrt(2.0))
    t = 1.0 / (1.0 + 0.3275911 * z)
    expo = jnp.exp(-0.5 * x * x)
    poly = t * (
        0.254829592
        + t * (-0.284496736 + t * (1.421413741 + t * (-1.453152027 + t * 1.061405429)))
    )
    tail = 0.5 * poly * expo
    cdf = jnp.where(x >= 0, 1.0 - tail, tail)
    return x * cdf, cdf + x * (expo * (1.0 / math.sqrt(2.0 * math.pi)))


def remote(src, dst, send, recv, dev):
    return pltpu.make_async_remote_copy(
        src_ref=src, dst_ref=dst, send_sem=send, recv_sem=recv, device_id=dev, device_id_type=MESH
    )


class Net:
    def __init__(self, fsdp):
        self.fsdp = fsdp
        self.half = fsdp // 2
        self.f = f = lax.axis_index("fsdp")
        self.t = t = lax.axis_index("tp")
        self.pf = f + 1 - 2 * lax.rem(f, 2)
        self.t2 = lax.rem(t + 2, 4)
        self.s = t + 1 - 2 * lax.rem(t, 2)
        self.s2 = lax.rem(self.s + 2, 4)
        self.partner = (self.pf, t)
        self.across = (f, self.t2)
        self.sibling = (f, self.s)

    def at(self, base, k):
        return lax.rem(base + 2 * k + self.fsdp, self.fsdp)

    def line(self, k):
        return (self.at(self.f, k), self.t)

    def barrier(self):
        sem = pltpu.get_barrier_semaphore()
        peers = [self.partner, self.across, self.sibling]
        peers += [self.line(k) for k in range(1, self.half)]
        for peer in peers:
            pl.semaphore_signal(sem, inc=1, device_id=peer, device_id_type=MESH)
        pl.semaphore_wait(sem, len(peers))


class Gather:
    def __init__(self, net, block, sems, unit):
        self.net, self.block, self.unit = net, block, unit
        self.ps, self.pr, self.ls, self.lr = sems

    def _pair(self, j, k):
        u = self.unit
        return remote(self.block(j), self.block(j), self.ps.at[u, k], self.pr.at[u, k], self.net.partner)

    def _line(self, j, k):
        u = self.unit
        return remote(self.block(j), self.block(j), self.ls.at[u, k], self.lr.at[u, k], self.net.line(k))

    def start(self):
        n = self.net
        for k in range(1, n.half):
            self._line(n.f, k).start()
        self._pair(n.f, 0).start()

    def forward(self):
        n = self.net
        for k in range(1, n.half):
            j = n.at(n.f, -k)
            self._line(j, k).wait_recv()
            self._pair(j, k).start()

    def finish(self):
        n = self.net
        for k in range(n.half):
            self._pair(n.at(n.pf, -k), k).wait_recv()

    def drain(self):
        n = self.net
        for k in range(n.half):
            self._pair(n.f, k).wait_send()
        for k in range(1, n.half):
            self._line(n.f, k).wait_send()


class Reduce:
    def __init__(self, net, block, first, second, sems, unit):
        self.net, self.block, self.first, self.second, self.unit = net, block, first, second, unit
        self.ps, self.pr, self.ls, self.lr = sems

    def _pair(self, k):
        n, u = self.net, self.unit
        return remote(
            self.block(n.at(n.pf, k)), self.first(k), self.ps.at[u, k], self.pr.at[u, k], n.partner
        )

    def _line(self, k):
        n, u = self.net, self.unit
        return remote(
            self.block(n.at(n.f, k)), self.second(k), self.ls.at[u, k], self.lr.at[u, k], n.line(k)
        )

    def start(self):
        for k in list(range(1, self.net.half)) + [0]:
            self._pair(k).start()

    def middle(self):
        n = self.net
        for k in range(1, n.half):
            self._pair(k).wait_recv()
            mine = self.block(n.at(n.f, k))
            mine[...] = (mine[...].astype(F32) + self.first(k)[...].astype(F32)).astype(BF)
            self._line(k).start()

    def finish(self):
        n = self.net
        self._pair(0).wait_recv()
        total = self.block(n.f)[...].astype(F32) + self.first(0)[...].astype(F32)
        for k in range(1, n.half):
            self._line(k).wait_recv()
            total = total + self.second(k)[...].astype(F32)
        return total

    def drain(self):
        for k in range(self.net.half):
            self._pair(k).wait_send()
        for k in range(1, self.net.half):
            self._line(k).wait_send()


class RowGather:
    def __init__(self, net, block, sems, unit):
        self.net, self.block, self.unit = net, block, unit
        self.ys, self.yr, self.cs, self.cr = sems

    def _y(self, j):
        u = self.unit
        return remote(self.block(j), self.block(j), self.ys.at[u], self.yr.at[u], self.net.across)

    def _c(self, j, k):
        u = self.unit
        return remote(self.block(j), self.block(j), self.cs.at[u, k], self.cr.at[u, k], self.net.sibling)

    def start(self):
        self._y(self.net.t).start()
        self._c(self.net.t, 0).start()

    def forward(self):
        n = self.net
        self._y(n.t2).wait_recv()
        self._c(n.t2, 1).start()

    def finish(self):
        n = self.net
        self._c(n.s, 0).wait_recv()
        self._c(n.s2, 1).wait_recv()

    def drain(self):
        n = self.net
        self._y(n.t).wait_send()
        self._c(n.t, 0).wait_send()
        self._c(n.t2, 1).wait_send()


class RowReduce:
    def __init__(self, net, block, first, second, sems, unit):
        self.net, self.block, self.first, self.second, self.unit = net, block, first, second, unit
        self.ys, self.yr, self.cs, self.cr = sems

    def _c(self, k):
        n, u = self.net, self.unit
        j = n.s2 if k == 0 else n.s
        return remote(self.block(j), self.first(k), self.cs.at[u, k], self.cr.at[u, k], n.sibling)

    def _y(self):
        n, u = self.net, self.unit
        return remote(self.block(n.t2), self.second(), self.ys.at[u], self.yr.at[u], n.across)

    def start(self):
        self._c(0).start()
        self._c(1).start()

    def middle(self, add=None):
        n = self.net
        self._c(0).wait_recv()
        mine = self.block(n.t2)
        if add is None:
            mine[...] = (mine[...].astype(F32) + self.first(0)[...].astype(F32)).astype(BF)
        else:
            add(mine, self.first(0))
        self._y().start()

    def finish(self):
        n = self.net
        self._c(1).wait_recv()
        self._y().wait_recv()
        return (
            self.block(n.t)[...].astype(F32)
            + self.first(1)[...].astype(F32)
            + self.second()[...].astype(F32)
        )

    def drain(self):
        self._c(0).wait_send()
        self._c(1).wait_send()
        self._y().wait_send()


def head_masks(rows, width):
    lane = lax.broadcasted_iota(jnp.int32, (rows, width), 1)
    return [
        (lane >= h * HEAD_DIM) & (lane < (h + 1) * HEAD_DIM) for h in range(width // HEAD_DIM)
    ]


def stack_heads(rows, masks):
    zero = jnp.zeros_like(rows)
    return jnp.concatenate([jnp.where(mask, rows, zero) for mask in masks], axis=0)


def merge_heads(stacked, masks):
    count = masks[0].shape[0]
    total = jnp.where(masks[0], stacked[:count], 0.0)
    for h in range(1, len(masks)):
        total = jnp.where(masks[h], stacked[h * count : (h + 1) * count], total)
    return total


def front_kernel(fsdp, early, *refs):
    it = iter(refs)
    take = lambda n: [next(it) for _ in range(n)]
    cnt, x_in, dy_in, par_in, aw_in, w1_in, w2_in = take(7)
    xg, dyg, rin, qkv, prob, mix, hid, n2g, awg, par, wg = take(11)
    parg, part, first, second = take(4)
    ga = take(4)
    rg = take(4)
    rr = take(4)
    (loc,) = take(1)
    net = Net(fsdp)
    f, t = net.f, net.t
    rows, width = x_in.shape[1], x_in.shape[2]
    images = xg.shape[0] // 2
    hw = qkv.shape[3]
    own = width // fsdp

    gat_par = Gather(net, lambda j: parg.at[j], ga, 0)
    gat_aw = Gather(net, lambda j: awg.at[j], ga, 1)
    gat_e = [Gather(net, (lambda e: lambda j: wg.at[e, j])(e), ga, 2 + e) for e in range(early)]
    row_x = [RowGather(net, (lambda m: lambda j: xg.at[m * images + j])(m), rg, m) for m in range(2)]
    row_dy = [RowGather(net, (lambda m: lambda j: dyg.at[m * images + j])(m), rg, 2 + m) for m in range(2)]
    row_n2 = [RowGather(net, (lambda m: lambda j: n2g.at[m * images + j])(m), rg, 4 + m) for m in range(2)]
    red = [
        RowReduce(
            net,
            (lambda m: lambda j: part.at[m, j])(m),
            (lambda m: lambda k: first.at[m, k])(m),
            (lambda m: lambda: second.at[m])(m),
            rr,
            m,
        )
        for m in range(2)
    ]

    copies = []
    for e in range(early):
        for i, src in enumerate((w1_in, w2_in)):
            copies.append(pltpu.make_async_copy(src.at[e], wg.at[e, f, i], loc.at[2 * e + i]))
    for copy in copies:
        copy.start()
    parg[f] = par_in[...]
    awg[f] = aw_in[...]
    for m in range(2):
        xg[m * images + t] = x_in[m]
        dyg[m * images + t] = dy_in[m]
    net.barrier()
    gat_par.start()
    row_x[0].start()
    gat_aw.start()
    row_x[1].start()
    for copy in copies:
        copy.wait()
    if early:
        gat_e[0].start()
    gat_par.forward()
    for m in range(2):
        row_dy[m].start()
    gat_aw.forward()
    row_x[0].forward()
    gat_par.finish()

    place = lax.broadcasted_iota(jnp.int32, (128, width), 0)
    column = lax.broadcasted_iota(jnp.int32, (128, width), 1)
    joined = jnp.zeros((16, width), F32)
    for j in range(fsdp):
        hot = ((column == place + j * own) & (place < own)).astype(BF)
        joined = joined + dot_nn(parg[j], hot)
    par[...] = joined
    gain_one, shift_one = par[0:1, :], par[1:2, :]
    mix_bias, gain_two, shift_two = par[2:3, :], par[3:4, :], par[4:5, :]

    def first_norm(i, carry):
        normed, _ = norm_parts(xg[i].astype(F32))
        rin[i] = (normed * gain_one + shift_one).astype(BF)
        return carry

    row_x[0].finish()
    lax.fori_loop(0, images, first_norm, 0)
    row_x[1].forward()
    if early:
        gat_e[0].forward()
    if early > 1:
        gat_e[1].start()
    row_x[1].finish()
    lax.fori_loop(images, 2 * images, first_norm, 0)
    gat_aw.finish()

    weights = awg[...].reshape(width, 4 * hw)
    for m in range(2):
        block = rin[m * images : (m + 1) * images].reshape(images * rows, width)
        for c in range(3):
            made = dot_nn(block, weights[:, c * hw : (c + 1) * hw])
            qkv[c, m * images : (m + 1) * images] = made.astype(BF).reshape(images, rows, hw)
    for m in range(2):
        row_dy[m].forward()
    masks = head_masks(rows, hw)
    key_pos = lax.broadcasted_iota(jnp.int32, (len(masks) * rows, rows), 1)

    def attend(i, carry):
        stacked = stack_heads(qkv[0, i], masks)
        scores = dot_nt(stacked, qkv[1, i]) * (1.0 / math.sqrt(HEAD_DIM))
        scores = jnp.where(key_pos < cnt[i], scores, MASK_FILL)
        expo = jnp.exp(scores - jnp.max(scores, axis=-1, keepdims=True))
        probs = (expo / jnp.sum(expo, axis=-1, keepdims=True)).astype(BF)
        prob[i] = probs
        mix[i] = merge_heads(dot_nn(probs, qkv[2, i]), masks).astype(BF)
        return carry

    out_w = awg[...].reshape(width, 4 * hw)[:, 3 * hw :]
    for m in range(2):
        lax.fori_loop(m * images, (m + 1) * images, attend, 0)
        block = mix[m * images : (m + 1) * images].reshape(images * rows, hw)
        part[m] = dot_nt(block, out_w).astype(BF).reshape(images, rows, width)
        red[m].start()
        if m == 0:
            red[0].middle()
            for e in range(1, early):
                gat_e[e].forward()
                if e + 1 < early:
                    gat_e[e + 1].start()
    red[1].middle()
    for m in range(2):
        hidden = x_in[m].astype(F32) + red[m].finish() + mix_bias
        hid[m] = hidden
        normed, _ = norm_parts(hidden)
        n2g[m * images + t] = (normed * gain_two + shift_two).astype(BF)
        row_n2[m].start()
    for m in range(2):
        row_n2[m].forward()
        row_dy[m].finish()
    for m in range(2):
        row_n2[m].finish()
    for e in range(early):
        gat_e[e].finish()
    for op in [gat_par, gat_aw] + gat_e + row_x + row_dy + row_n2 + red:
        op.drain()


def expert_kernel(fsdp, early, reduce_early, *refs):
    it = iter(refs)
    take = lambda n: [next(it) for _ in range(n)]
    n2g, dyg, par, wearly, w1_in, w2_in, b1, route, prio = take(9)
    total, gout, glate, hb, ob = take(5)
    wbuf, acc, hot_s, xs, vs, gas, dps, sid, rp, part, first, second, r1, r2 = take(14)
    ga = take(4)
    rs = take(4)
    rr = take(4)
    loc, late_sem = take(2)
    net = Net(fsdp)
    f, t = net.f, net.t
    experts, slots = wbuf.shape[0], hot_s.shape[1]
    rows, width = n2g.shape[1], n2g.shape[2]
    images = n2g.shape[0] // 2
    full = images * rows
    ff = wbuf.shape[4]
    late = experts - early

    def gather(e):
        return Gather(net, lambda j: wbuf.at[e, j], ga, e - early)

    def reduce(e):
        return Reduce(
            net,
            lambda j: wbuf.at[e, j],
            lambda k: r1.at[e, k],
            lambda k: r2.at[e, k],
            rs,
            e,
        )

    copies = []
    for e in range(early):
        copies.append(pltpu.make_async_copy(wearly.at[e], wbuf.at[e], loc.at[e]))
    own_copies = []
    for e in range(early, experts):
        for i, src in enumerate((w1_in, w2_in)):
            own_copies.append(
                pltpu.make_async_copy(src.at[e], wbuf.at[e, f, i], loc.at[experts + 2 * e + i])
            )
    for copy in own_copies + copies:
        copy.start()
    net.barrier()
    for copy in own_copies:
        copy.wait()
    if late:
        gather(early).start()

    for m in range(2):
        e0, e1, order = route[m, 0:1, :], route[m, 1:2, :], route[m, 2:3, :]
        lower = (prio[m] < order).astype(BF)
        kind = lax.broadcasted_iota(jnp.int32, (16, full), 0)
        named = jnp.where(kind < experts, e0, e1) == jnp.where(kind < experts, kind, kind - experts)
        named = jnp.where((kind < 2 * experts) & named, 1.0, 0.0)
        counts = dot_nn(named.astype(BF), lower)
        totals = jnp.sum(named, axis=1, keepdims=True)
        for k in range(2):
            mine = jnp.zeros((1, full), F32)
            where_slot = jnp.full((1, full), -1.0, F32)
            for e in range(experts):
                c = k * experts + e
                before = counts[c : c + 1, :]
                if k == 1:
                    before = before + totals[e : e + 1, :]
                kept = (named[c : c + 1, :] > 0.5) & (before < slots)
                where_slot = jnp.where(kept, before + e * slots, where_slot)
            sid[m, k : k + 1, :] = where_slot.astype(jnp.int32)
        n2m = n2g[m * images : (m + 1) * images].reshape(full, width)
        logits = dot_nt(par[...].astype(BF), n2m)[5 : 5 + experts, :]
        expo = jnp.exp(logits - jnp.max(logits, axis=0, keepdims=True))
        rp[m, 0:experts, :] = expo / jnp.sum(expo, axis=0, keepdims=True)
        acc[m] = jnp.zeros_like(acc[m])
    hb[...] = jnp.zeros_like(hb)
    ob[...] = jnp.zeros_like(ob)
    for copy in copies:
        copy.wait()

    slot_row = lax.broadcasted_iota(jnp.int32, (slots, full), 0)
    lane = lax.broadcasted_iota(jnp.int32, (slots, 128), 1)

    def expert(e, carry):
        if late:

            @pl.when((e + 1 >= early) & (e + 1 < experts) & (e + 1 > early))
            def _():
                gather(e + 1).start()

        gates = []
        for m in range(2):
            hot = (slot_row + e * slots == sid[m, 0:1, :]) | (slot_row + e * slots == sid[m, 1:2, :])
            hot_s[m] = jnp.where(hot, 1.0, 0.0).astype(BF)
            gates.append(
                jnp.sum(jnp.where(hot, rp[m, pl.ds(e, 1), :], 0.0), axis=1, keepdims=True)
            )
            n2m = n2g[m * images : (m + 1) * images].reshape(full, width)
            dym = dyg[m * images : (m + 1) * images].reshape(full, width)
            xs[m] = dot_nn(hot_s[m], n2m).astype(BF)
            vals = dot_nn(hot_s[m], dym)
            ob[pl.ds(e, 1), :] += jnp.sum(gates[m] * vals, axis=0, keepdims=True)
            vs[m] = vals.astype(BF)
        if late:

            @pl.when(e >= early)
            def _():
                gather(e).forward()
                gather(e).finish()

        w1 = wbuf[e, :, 0].reshape(width, ff)
        w2 = wbuf[e, :, 1].reshape(width, ff)
        for m in range(2):
            pre = dot_nn(xs[m], w1) + b1[pl.ds(e, 1), :]
            act, slope = gelu_parts(pre)
            gas[m] = (gates[m] * act).astype(BF)
            back = dot_nn(vs[m], w2)
            d_gate = jnp.sum(act * back, axis=1, keepdims=True)
            d_pre = gates[m] * slope * back
            hb[pl.ds(e, 1), :] += jnp.sum(d_pre, axis=0, keepdims=True)
            dps[m] = d_pre.astype(BF)
            high = d_gate.astype(BF)
            low = (d_gate - high.astype(F32)).astype(BF)
            zero = jnp.zeros((slots, 128), BF)
            made = [dot_nt(gas[m], w2).astype(BF), dot_nt(dps[m], w1).astype(BF)]
            made.append(
                jnp.where(lane == e, high, jnp.where(lane == 16 + e, jnp.ones_like(zero), zero))
            )
            made.append(jnp.where(lane == e, low, zero))
            acc[m] += dot_tn(hot_s[m], jnp.concatenate(made, axis=1))
        if late:

            @pl.when(e >= early)
            def _():
                gather(e).drain()

        two = 2 * slots
        wbuf[e, :, 0] = (
            dot_tn(xs[...].reshape(two, width), dps[...].reshape(two, ff))
            .astype(BF)
            .reshape(fsdp, width // fsdp, ff)
        )
        wbuf[e, :, 1] = (
            dot_tn(vs[...].reshape(two, width), gas[...].reshape(two, ff))
            .astype(BF)
            .reshape(fsdp, width // fsdp, ff)
        )
        if reduce_early:

            @pl.when(e < reduce_early)
            def _():
                reduce(e).start()

            @pl.when((e >= 1) & (e <= reduce_early))
            def _():
                reduce(e - 1).middle()

        if reduce_early < experts:

            @pl.when(e >= reduce_early)
            def _():
                pltpu.make_async_copy(
                    wbuf.at[e], glate.at[e - reduce_early], late_sem.at[e - reduce_early]
                ).start()

        return carry

    lax.fori_loop(0, experts, expert, 0)

    red = [
        RowReduce(
            net,
            (lambda m: lambda j: part.at[m, j])(m),
            (lambda m: lambda k: first.at[m, k])(m),
            (lambda m: lambda: second.at[m])(m),
            rr,
            m,
        )
        for m in range(2)
    ]
    wide = 2 * width

    def add_split(mine, other):
        mine[:, :wide] = (mine[:, :wide].astype(F32) + other[:, :wide].astype(F32)).astype(BF)
        pair = [mine[:, wide : wide + 128].astype(F32), mine[:, wide + 128 :].astype(F32)]
        pair += [other[:, wide : wide + 128].astype(F32), other[:, wide + 128 :].astype(F32)]
        value = (pair[0] + pair[2]) + (pair[1] + pair[3])
        high = value.astype(BF)
        mine[:, wide : wide + 128] = high
        mine[:, wide + 128 :] = (value - high.astype(F32)).astype(BF)

    for m in range(2):
        part[m, :, :, :wide] = acc[m, :, :wide].astype(BF).reshape(images, rows, wide)
        value = acc[m, :, wide : wide + 128] + acc[m, :, wide + 128 :]
        high = value.astype(BF)
        part[m, :, :, wide : wide + 128] = high.reshape(images, rows, 128)
        part[m, :, :, wide + 128 :] = (value - high.astype(F32)).astype(BF).reshape(images, rows, 128)
        red[m].start()
    for m in range(2):
        red[m].middle(add_split)
    if reduce_early == experts:
        reduce(experts - 1).middle()
    for e in range(reduce_early):
        gout[e] = reduce(e).finish()
        reduce(e).drain()
    for m in range(2):
        total[m] = red[m].finish()
        red[m].drain()
    for e in range(reduce_early, experts):
        pltpu.make_async_copy(
            wbuf.at[e], glate.at[e - reduce_early], late_sem.at[e - reduce_early]
        ).wait()


def back_kernel(fsdp, experts, *refs):
    it = iter(refs)
    take = lambda n: [next(it) for _ in range(n)]
    total, hid, n2g, dy_in, x_in, xg, rin, qkv, prob, mix, awg, par, gl, hb, ob = take(15)
    y_out, gx_out, ga_out, gl_out, small = take(5)
    hlg, dmx, dpj, dh, gaw, part, first, second, r1, r2, a1, a2, z1, z2, z3, z4, zs = take(17)
    rs = take(4)
    rg = take(4)
    rr = take(4)
    sm_s, sm_r = take(2)
    net = Net(fsdp)
    f, t = net.f, net.t
    rows, width = hid.shape[1], hid.shape[2]
    images = n2g.shape[0] // 2
    full = images * rows
    hw = qkv.shape[3]
    live = y_out.shape[1]
    late = gl.shape[0]
    wide = 2 * width
    scale = 1.0 / math.sqrt(HEAD_DIM)

    red_g = [
        Reduce(
            net,
            (lambda e: lambda j: gl.at[e, j])(e),
            (lambda e: lambda k: r1.at[e, k])(e),
            (lambda e: lambda k: r2.at[e, k])(e),
            rs,
            e,
        )
        for e in range(late)
    ]
    red_a = Reduce(net, lambda j: gaw.at[j], lambda k: a1.at[k], lambda k: a2.at[k], rs, late)
    row_h = [RowGather(net, (lambda m: lambda j: hlg.at[m * images + j])(m), rg, m) for m in range(2)]
    red = [
        RowReduce(
            net,
            (lambda m: lambda j: part.at[m, j])(m),
            (lambda m: lambda k: first.at[m, k])(m),
            (lambda m: lambda: second.at[m])(m),
            rr,
            m,
        )
        for m in range(2)
    ]
    net.barrier()
    for op in red_g:
        op.start()

    gain_one, gain_two = par[0:1, :], par[3:4, :]
    shift_two = par[4:5, :]
    zs[...] = jnp.zeros_like(zs)
    lane = lax.broadcasted_iota(jnp.int32, (rows, 128), 1)
    lane16 = lax.broadcasted_iota(jnp.int32, (rows, 16), 1)
    router_lane = (lane16 >= 5) & (lane16 < 5 + experts)
    for m in range(2):
        hidden = hid[m]
        normed, inv = norm_parts(hidden)
        dy = dy_in[m].astype(F32)
        n2 = n2g[m * images + t]
        logits = jnp.where(router_lane, dot_nt(n2, par[...].astype(BF)), -1e30)
        expo = jnp.exp(logits - jnp.max(logits, axis=1, keepdims=True))
        probs = expo / jnp.sum(expo, axis=1, keepdims=True)
        sums = total[m, :, wide : wide + 128] + total[m, :, wide + 128 :]
        pcol, qcol, out = [], [], hidden + total[m, :, :width]
        for e in range(experts):
            p_e = jnp.sum(jnp.where(lane16 == 5 + e, probs, 0.0), axis=1, keepdims=True)
            kept = 0.25 * jnp.sum(jnp.where(lane == 16 + e, sums, 0.0), axis=1, keepdims=True)
            q_e = jnp.sum(jnp.where(lane == e, sums, 0.0), axis=1, keepdims=True)
            bias = par[5 + experts + e : 6 + experts + e, :]
            q_e = q_e + kept * jnp.sum(dy * bias, axis=1, keepdims=True)
            out = out + (kept * p_e) * bias
            pcol.append(p_e)
            qcol.append(q_e)
        y_out[m] = out[:live]
        mean_q = pcol[0] * qcol[0]
        for e in range(1, experts):
            mean_q = mean_q + pcol[e] * qcol[e]
        mid = total[m, :, width:wide]
        for e in range(experts):
            d_logit = (pcol[e] * (qcol[e] - mean_q)).astype(BF).astype(F32)
            mid = mid + d_logit * par[5 + e : 6 + e, :]
            zs[5 + e : 6 + e, :] += jnp.sum(d_logit * n2.astype(F32), axis=0, keepdims=True)
        d_hidden = dy + norm_back(mid * gain_two, normed, inv)
        dh[m] = d_hidden
        hlg[m * images + t] = d_hidden.astype(BF)
        row_h[m].start()
        zs[2:3, :] += jnp.sum(d_hidden, axis=0, keepdims=True)
        zs[3:4, :] += jnp.sum(mid * normed, axis=0, keepdims=True)
        zs[4:5, :] += jnp.sum(mid, axis=0, keepdims=True)
    zs[5 + experts : 5 + 2 * experts, :] = 0.25 * ob[0:experts, :]
    zs[16 : 16 + experts, :] = hb[0:experts, :]
    for m in range(2):
        row_h[m].forward()

    masks = head_masks(rows, hw)
    weights = awg[...].reshape(width, 4 * hw)

    def attend_back(i, carry):
        stacked_d = stack_heads(dmx[i], masks)
        stacked_q = stack_heads(qkv[0, i], masks)
        probs_low = prob[i]
        probs = probs_low.astype(F32)
        d_prob = dot_nt(stacked_d, qkv[2, i])
        d_score = probs * (d_prob - jnp.sum(probs * d_prob, axis=-1, keepdims=True))
        d_score = d_score.astype(BF)
        dpj[0, i] = (merge_heads(dot_nn(d_score, qkv[1, i]), masks) * scale).astype(BF)
        dpj[1, i] = (dot_tn(d_score, stacked_q) * scale).astype(BF)
        dpj[2, i] = dot_tn(probs_low, stacked_d).astype(BF)
        return carry

    for m in range(2):
        row_h[m].finish()
        span = slice(m * images, (m + 1) * images)
        block = hlg[span].reshape(full, width)
        dmx[span] = dot_nn(block, weights[:, 3 * hw :]).astype(BF).reshape(images, rows, hw)
        lax.fori_loop(m * images, (m + 1) * images, attend_back, 0)
        low = jnp.zeros((full, width), F32)
        for c in range(3):
            low = low + dot_nt(dpj[c, span].reshape(full, hw), weights[:, c * hw : (c + 1) * hw])
        part[m] = low.astype(BF).reshape(images, rows, width)
        red[m].start()
        if m == 0:
            for op in red_g:
                op.middle()
        red[m].middle()

    flat_in = rin[...].reshape(2 * full, width)
    flat_h = hlg[...].reshape(2 * full, width)
    made = [dot_tn(flat_in, dpj[c].reshape(2 * full, hw)) for c in range(3)]
    made.append(dot_tn(flat_h, mix[...].reshape(2 * full, hw)))
    gaw[...] = jnp.concatenate(made, axis=1).astype(BF).reshape(fsdp, width // fsdp, 4 * hw)
    red_a.start()
    for m in range(2):
        low = red[m].finish()
        normed, inv = norm_parts(x_in[m].astype(F32))
        gx_out[m] = (dh[m] + norm_back(low * gain_one, normed, inv))[:live]
        zs[0:1, :] += jnp.sum(low * normed, axis=0, keepdims=True)
        zs[1:2, :] += jnp.sum(low, axis=0, keepdims=True)
    red_a.middle()

    hops = [(z1, 0, net.sibling), (z2, 1, net.across), (z3, 2, net.partner)]
    for buf, i, dev in hops:
        part_of = slice(0, 16) if i < 2 else slice(0, 24)
        src = zs.at[part_of]
        copy = remote(src, buf, sm_s.at[i], sm_r.at[i], dev)
        copy.start()
        copy.wait()
        zs[part_of] = zs[part_of] + buf[...]
    for k in range(1, net.half):
        remote(zs, z4.at[k], sm_s.at[2 + k], sm_r.at[2 + k], net.line(k)).start()
    for e in range(late):
        gl_out[e] = red_g[e].finish()
    ga_out[...] = red_a.finish()
    sums = zs[...]
    for k in range(1, net.half):
        remote(zs, z4.at[k], sm_s.at[2 + k], sm_r.at[2 + k], net.line(k)).wait()
        sums = sums + z4[k]
    small[...] = sums
    for op in red_g + [red_a] + row_h + red:
        op.drain()


def vmem(shape, dtype=BF):
    return pltpu.VMEM(shape, dtype)


def spec(space):
    return pl.BlockSpec(memory_space=space)


V = pltpu.VMEM
H = pltpu.HBM


def pair_sems(units, half):
    return [DMA((units, half)) for _ in range(4)]


def row_sems(units):
    return [DMA((units,)), DMA((units,)), DMA((units, 2)), DMA((units, 2))]


def per_device(
    patch_embeddings,
    upstream_gradient,
    picture_valid_count,
    assigned_specialists,
    filling_sequence_place,
    leading_scale_factor,
    leading_offset_vector,
    query_value_matrix,
    mixing_projection_matrix,
    mixing_offset_vector,
    central_scale_factor,
    central_offset_vector,
    gating_projection,
    specialist_widen_matrix,
    specialist_inner_offset,
    specialist_contract_matrix,
    specialist_final_offset,
):
    fsdp = lax.axis_size("fsdp")
    half = fsdp // 2
    tp = lax.axis_size("tp")
    own_rows, width = patch_embeddings.shape[1:]
    rows = -(-own_rows // 16) * 16
    images = tp
    full = images * rows
    own = leading_scale_factor.shape[0]
    hw = query_value_matrix.shape[2]
    heads = hw // HEAD_DIM
    experts, _, ff = specialist_widen_matrix.shape
    slots = 2 * own_rows * tp // experts
    early = min(EARLY_GATHER, experts)
    red_early = min(EARLY_REDUCE, experts)
    late = experts - early
    late_red = experts - red_early
    f_index = lax.axis_index("fsdp")

    pad_rows = ((0, 0), (0, rows - own_rows), (0, 0))
    x_own = jnp.pad(patch_embeddings, pad_rows)
    dy_own = jnp.pad(upstream_gradient, pad_rows)
    counts = picture_valid_count.reshape(2 * images)
    small_par = jnp.concatenate(
        [
            leading_scale_factor[None],
            leading_offset_vector[None],
            mixing_offset_vector[None],
            central_scale_factor[None],
            central_offset_vector[None],
            gating_projection.T,
            specialist_final_offset,
        ]
    )
    small_par = jnp.pad(small_par, ((0, 16 - small_par.shape[0]), (0, 128 - own)))
    att_w = jnp.concatenate(
        [query_value_matrix.reshape(own, 3 * hw), mixing_projection_matrix.T], axis=1
    )
    w1 = specialist_widen_matrix
    w2 = specialist_contract_matrix.transpose(0, 2, 1)
    by_image = lambda a, fill: jnp.pad(
        a.reshape(2, -1, images, own_rows),
        ((0, 0), (0, 0), (0, 0), (0, rows - own_rows)),
        constant_values=fill,
    ).reshape(2, -1, full)
    prio_row = by_image(filling_sequence_place, own_rows * tp)
    route = jnp.concatenate(
        [
            by_image(assigned_specialists.transpose(0, 2, 1), -1),
            prio_row,
            jnp.zeros((2, 5, full), jnp.int32),
        ],
        axis=1,
    )
    prio_col = prio_row.reshape(2, full, 1)
    inner = jnp.pad(specialist_inner_offset.astype(F32), ((0, 8 - experts), (0, 0)))

    params = lambda cid: pltpu.CompilerParams(
        collective_id=cid, has_side_effects=True, vmem_limit_bytes=VMEM_LIMIT
    )
    sds = jax.ShapeDtypeStruct
    xg, dyg, rin, qkv, prob, mix, hid, n2g, awg, par, wearly = pl.pallas_call(
        functools.partial(front_kernel, fsdp, early),
        out_shape=[
            sds((2 * images, rows, width), BF),
            sds((2 * images, rows, width), BF),
            sds((2 * images, rows, width), BF),
            sds((3, 2 * images, rows, hw), BF),
            sds((2 * images, heads * rows, rows), BF),
            sds((2 * images, rows, hw), BF),
            sds((2, rows, width), F32),
            sds((2 * images, rows, width), BF),
            sds((fsdp, own, 4 * hw), BF),
            sds((16, width), F32),
            sds((max(early, 1), fsdp, 2, own, ff), BF),
        ],
        in_specs=[spec(pltpu.SMEM), spec(V), spec(V), spec(V), spec(V), spec(H), spec(H)],
        out_specs=[spec(V)] * 10 + [spec(H)],
        scratch_shapes=[
            vmem((fsdp, 16, 128)),
            vmem((2, images, rows, width)),
            vmem((2, 2, rows, width)),
            vmem((2, rows, width)),
        ]
        + pair_sems(2 + early, half)
        + row_sems(6)
        + row_sems(2)
        + [DMA((2 * experts,))],
        compiler_params=params(1),
        name="front",
    )(counts, x_own, dy_own, small_par, att_w, w1, w2)

    wide = 2 * width + 256
    total, gout, glate, hb, ob = pl.pallas_call(
        functools.partial(expert_kernel, fsdp, early, red_early),
        out_shape=[
            sds((2, rows, wide), F32),
            sds((max(red_early, 1), 2, own, ff), F32),
            sds((max(late_red, 1), fsdp, 2, own, ff), BF),
            sds((8, ff), F32),
            sds((8, width), F32),
        ],
        in_specs=[spec(V), spec(V), spec(V), spec(H), spec(H), spec(H), spec(V), spec(V), spec(V)],
        out_specs=[spec(V), spec(V), spec(H), spec(V), spec(V)],
        scratch_shapes=[
            vmem((experts, fsdp, 2, own, ff)),
            vmem((2, full, wide), F32),
            vmem((2, slots, full)),
            vmem((2, slots, width)),
            vmem((2, slots, width)),
            vmem((2, slots, ff)),
            vmem((2, slots, ff)),
            vmem((2, 8, full), jnp.int32),
            vmem((2, 8, full), F32),
            vmem((2, images, rows, wide)),
            vmem((2, 2, rows, wide)),
            vmem((2, rows, wide)),
            vmem((max(red_early, 1), half, 2, own, ff)),
            vmem((max(red_early, 1), half, 2, own, ff)),
        ]
        + pair_sems(max(late, 1), half)
        + pair_sems(max(red_early, 1), half)
        + row_sems(2)
        + [DMA((3 * experts,)), DMA((max(late_red, 1),))],
        compiler_params=params(2),
        name="experts",
    )(n2g, dyg, par, wearly, w1, w2, inner, route, prio_col)

    y_out, gx_out, ga_out, gl_out, small = pl.pallas_call(
        functools.partial(back_kernel, fsdp, experts),
        out_shape=[
            sds((2, own_rows, width), F32),
            sds((2, own_rows, width), F32),
            sds((own, 4 * hw), F32),
            sds((late_red, 2, own, ff), F32),
            sds((24, width), F32),
        ],
        in_specs=[spec(V)] * 15,
        out_specs=[spec(V)] * 5,
        scratch_shapes=[
            vmem((2 * images, rows, width)),
            vmem((2 * images, rows, hw)),
            vmem((3, 2 * images, rows, hw)),
            vmem((2, rows, width), F32),
            vmem((fsdp, own, 4 * hw)),
            vmem((2, images, rows, width)),
            vmem((2, 2, rows, width)),
            vmem((2, rows, width)),
            vmem((late_red, half, 2, own, ff)),
            vmem((late_red, half, 2, own, ff)),
            vmem((half, own, 4 * hw)),
            vmem((half, own, 4 * hw)),
            vmem((16, width), F32),
            vmem((16, width), F32),
            vmem((24, width), F32),
            vmem((half, 24, width), F32),
            vmem((24, width), F32),
        ]
        + pair_sems(late_red + 1, half)
        + row_sems(2)
        + row_sems(2)
        + [DMA((2 + half,)), DMA((2 + half,))],
        compiler_params=params(3),
        name="back",
    )(total, hid, n2g, dy_own, x_own, xg, rin, qkv, prob, mix, awg, par, glate, hb, ob)

    grads = jnp.concatenate([gout, gl_out], axis=0)
    cut = lax.dynamic_slice_in_dim(small, f_index * own, own, 1)
    return (
        y_out,
        gx_out,
        cut[0],
        cut[1],
        ga_out[:, : 3 * hw].reshape(own, 3, hw),
        ga_out[:, 3 * hw :].T,
        cut[2],
        cut[3],
        cut[4],
        cut[5 : 5 + experts].T,
        grads[:, 0],
        small[16 : 16 + experts],
        grads[:, 1].transpose(0, 2, 1),
        cut[5 + experts : 5 + 2 * experts],
    )


def solution(mesh):
    placed = (
        P(None, ("fsdp", "tp"), None),
        P(None, ("fsdp", "tp"), None),
        P(None, "fsdp"),
        P(None, "fsdp", None),
        P(None, "fsdp", None),
        P("fsdp"),
        P("fsdp"),
        P("fsdp", None, "tp"),
        P("tp", "fsdp"),
        P("fsdp"),
        P("fsdp"),
        P("fsdp"),
        P("fsdp", None),
        P(None, "fsdp", "tp"),
        P(None, "tp"),
        P(None, "tp", "fsdp"),
        P(None, "fsdp"),
    )
    return jax.shard_map(
        per_device,
        mesh=mesh,
        in_specs=placed,
        out_specs=(
            P(None, ("fsdp", "tp"), None),
            P(None, ("fsdp", "tp"), None),
            P("fsdp"),
            P("fsdp"),
            P("fsdp", None, "tp"),
            P("tp", "fsdp"),
            P("fsdp"),
            P("fsdp"),
            P("fsdp"),
            P("fsdp", None),
            P(None, "fsdp", "tp"),
            P(None, "tp"),
            P(None, "tp", "fsdp"),
            P(None, "fsdp"),
        ),
        check_vma=False,
    )
```

time: 1260 us -> 430 us (0.34)
  waiting for transfers between devices: 517 us -> 0 us
  Pallas kernels: 0 us -> 401 us
  local copies, waits for them, and re-layouts: 253 us -> 18.6 us
  blocking collectives: 196 us -> 0 us
  matrix products: 129 us -> 0 us
  other arithmetic: 131 us -> 2.09 us
  between operations: 17.8 us -> 1.36 us
    pallas_call x0 -> x3, Pallas kernels: none -> 401 us  [the longest x1 187 us: per_device(): pl.pallas_call(functools.partial(expert_kernel, fsdp, early, red_early),...]
    reduce_scatter x11 -> x0, waiting for transfers between devices: 342 us -> none  [the longest x1 96.5 us: per_device(): lax.psum_scatter(grad_expertw.astype(jnp.bfloat16), 'fsdp', scatter_dimen...]
    dot_general x42 -> x0, matrix products: 124 us -> none  [the longest x2 21.4 us: per_device(): jnp.einsum('ecd,efd->ecf', slot_low, expout_full, preferred_element_type=...]
    gather x14 -> x0, local copies, waits for them, and re-layouts: 118 us -> none  [the longest x4 34.2 us: per_device(): picked = expert_pad[slot_ids]]
    unnamed x27 -> x0, waiting for transfers between devices: 117 us -> none
    all_gather x4 -> x0, blocking collectives: 104 us -> none  [the longest x1 36.6 us: per_device(): lax.all_gather(query_value_matrix, 'fsdp', axis=0, tiled=True)]
    reduce_sum x27 -> x0, other arithmetic: 64.3 us -> none  [the longest x2 23.1 us: per_device(): gate_part = jnp.sum(picked * cot_f[:, None, :], axis=2)]
    all_gather x10 -> x0, waiting for transfers between devices: 57.8 us -> none  [the longest x1 42.9 us: per_device(): lax.all_gather(specialist_contract_matrix, 'fsdp', axis=2, tiled=True)]
  transfers between devices with their start and end apart: 24 -> 0, of which waited for: 14 -> 0; matrix products, arithmetic and copies ran while one was open for 36% -> 0% of each run, Pallas kernels for 0% -> 0%
where the time goes in v1:
time: 430 us; the launch traced here: 423 us
  Pallas kernels  401 us (93%)
  local copies, waits for them, and re-layouts  18.6 us (4%)
    pallas_call x1, Pallas kernels, per_device(): pl.pallas_call(functools.partial(expert_kernel, fsdp, early, red_early),...  187 us
    pallas_call x1, Pallas kernels, per_device(): pl.pallas_call(functools.partial(back_kernel, fsdp, experts), out_shape=[...  108 us
    pallas_call x1, Pallas kernels, per_device(): pl.pallas_call(functools.partial(front_kernel, fsdp, early), out_shape=[s...  106 us

profile of v1, /device:TPU:0, one launch (start us, length us, event | category | flops | bytes accessed | tf_op | source)
XLA Modules:
  0.0 423.0 jit_solution(790285993852305834)
XLA Ops:
  0.6 0.0 copy-start.5
  0.7 0.0 copy-start.6
  0.7 0.0 copy-start.12
  0.7 0.0 copy-start.13
  0.7 0.0 copy-start.14
  0.7 0.0 copy-start.15
  0.7 0.0 copy-start.16
  0.7 0.0 copy-start.10
  0.7 0.0 copy-start.11
  0.7 0.0 copy-start.17
  0.7 2.1 pad.25.refs_1_.refs_4_
  2.8 2.0 pad.26.refs_2_.refs_3_
  4.8 0.2 copy.35
  4.9 0.2 copy.37
  5.1 0.1 copy.36
  5.2 0.7 pad_maximum_fusion.refs_4_
  6.0 0.0 copy-done.14
  6.0 0.1 concatenate.12
  6.1 0.6 pad.27.refs_3_
  6.7 0.6 reshape.49.refs_0_
  7.3 106.1 %front.1 = (bf16[8,208,768]{2,1,0:T(8,128)(2,1)}, bf16[8,208,768]{2,1,0:T(8,128)(2,1)}, bf16[8,208,768]{2,1,0:T(8,128)(2,1)}, bf16[3,8,208,192]{3,2,1,0:T(8,128)...) custom-call(s32[8]{0:T(128)} %reshape.49.refs_0_, ...), custom_call_target="tpu_custom_call" | custom-call | tf_op jit(solution)/shard_map/front/pallas_call | solution.py:895
  113.5 0.0 copy-done.8
  113.5 0.1 reshape.53
  113.6 1.2 reshape_reshape.4.refs_8_
  114.8 0.1 reshape.54
  114.9 0.0 copy-done.7
  114.9 0.1 reshape.51
  115.0 0.1 reshape.52
  115.1 0.1 pad.34.clone
  115.2 0.7 add_add_fusion.refs_7_
  115.9 0.6 pad_convert_fusion.refs_6_
  116.5 187.1 %experts.1 = (f32[2,208,1792]{2,1,0:T(8,128)}, f32[2,2,96,768]{3,2,1,0:T(8,128)}, bf16[2,8,2,96,768]{4,3,2,1,0:T(8,128)(2,1)}, f32[8,768]{1,0:T(8,128)}, f32[8,768]{1,0:T(8,128)}) custom-call(bf16[8,208,768]{2,1,0:T(8,128)(2,1)} %get-tuple-element.35.refs_0_.refs_2_, bf16[8,208,768]{2,1,0:T(8,128)(2,1)} %get-tuple-element.36.refs_1_, ...), custom_call_target="tpu_custom_call" | custom-call | tf_op jit(solution)/shard_map/experts/pallas_call | solution.py:927
  303.7 107.7 %back.1 = (f32[2,200,768]{2,1,0:T(8,128)}, f32[2,200,768]{2,1,0:T(8,128)}, f32[96,768]{1,0:T(8,128)}, f32[2,2,96,768]{3,2,1,0:T(8,128)}, f32[24,768]{1,0:T(8,128)}) custom-call(f32[2,208,1792]{2,1,0:T(8,128)} %get-tuple-element.39.refs_0_, f32[2,208,768]{2,1,0:T(8,128)} %get-tuple-element.40.refs_1_, bf16[8,208,768]{2,1,0:T(8,128)(2,1)} %get-tuple-element.35.refs_0_.refs_2_, ...), custom_call_target="tpu_custom_call" | custom-call | tf_op jit(solution)/shard_map/back/pallas_call | solution.py:962
  411.4 0.1 constant_dynamic-update-slice_fusion.1
  411.5 1.2 copy-done.3
  412.7 0.1 constant_dynamic-update-slice_fusion
  412.8 0.0 copy-start.4
  412.8 0.0 copy-start.1
  412.8 1.6 slice_bitcast_fusion
  414.4 0.1 copy.39
  414.5 0.9 copy.40
  415.4 0.1 slice_bitcast_fusion.2
  415.5 0.7 copy.41
  416.2 1.4 fusion
  417.7 1.5 dynamic-slice_bitcast_fusion.1
  419.2 1.3 slice.45
  420.5 1.0 copy.45
  421.5 1.0 copy.46
  (25 shorter events, 0.1 us)
Async XLA Ops:
  0.6 4.1 copy-start.5
  0.7 4.4 %copy-start.6 = (bf16[192,96]{1,0:T(8,128)(2,1)S(1)}, bf16[192,96]{1,0:T(8,128)(2,1)}, u32[]{:S(2)}) copy-start(bf16[192,96]{1,0:T(8,128)(2,1)} %param.25) | copy-start | bytes 110596
  0.7 5.3 %copy-start.12 = (bf16[96]{0:T(256)(128)(2,1)S(1)}, bf16[96]{0:T(256)(128)(2,1)}, u32[]{:S(2)}) copy-start(bf16[96]{0:T(256)(128)(2,1)} %param.22) | copy-start | bytes 580
  0.7 5.3 %copy-start.13 = (bf16[96]{0:T(256)(128)(2,1)S(1)}, bf16[96]{0:T(256)(128)(2,1)}, u32[]{:S(2)}) copy-start(bf16[96]{0:T(256)(128)(2,1)} %param.23) | copy-start | bytes 580
  0.7 5.3 %copy-start.14 = (bf16[96]{0:T(256)(128)(2,1)S(1)}, bf16[96]{0:T(256)(128)(2,1)}, u32[]{:S(2)}) copy-start(bf16[96]{0:T(256)(128)(2,1)} %param.26) | copy-start | bytes 580
  0.7 5.3 %copy-start.15 = (bf16[96]{0:T(256)(128)(2,1)S(1)}, bf16[96]{0:T(256)(128)(2,1)}, u32[]{:S(2)}) copy-start(bf16[96]{0:T(256)(128)(2,1)} %param.27) | copy-start | bytes 580
  0.7 5.3 %copy-start.16 = (bf16[96]{0:T(256)(128)(2,1)S(1)}, bf16[96]{0:T(256)(128)(2,1)}, u32[]{:S(2)}) copy-start(bf16[96]{0:T(256)(128)(2,1)} %param.28) | copy-start | bytes 580
  0.7 5.3 %copy-start.10 = (bf16[96,4]{0,1:T(4,128)(2,1)S(1)}, bf16[96,4]{0,1:T(4,128)(2,1)}, u32[]{:S(2)}) copy-start(bf16[96,4]{0,1:T(4,128)(2,1)} %param.29) | copy-start | bytes 2308
  0.7 5.3 %copy-start.11 = (bf16[4,96]{1,0:T(4,128)(2,1)S(1)}, bf16[4,96]{1,0:T(4,128)(2,1)}, u32[]{:S(2)}) copy-start(bf16[4,96]{1,0:T(4,128)(2,1)} %param.33) | copy-start | bytes 2308
  0.7 6.0 %copy-start.17 = (s32[2,4]{1,0:T(2,128)S(1)}, s32[2,4]{1,0:T(2,128)}, u32[]{:S(2)}) copy-start(s32[2,4]{1,0:T(2,128)} %param.19) | copy-start | bytes 100
  2.8 110.7 %copy-start.8 = (s32[2,1,800]{2,1,0:T(1,128)S(1)}, s32[2,1,800]{2,1,0:T(1,128)}, u32[]{:S(2)}) copy-start(s32[2,1,800]{2,1,0:T(1,128)} %param.21) | copy-start | bytes 19204
  4.8 110.2 %copy-start.7 = (s32[2,800,2]{1,2,0:T(2,128)S(1)}, s32[2,800,2]{1,2,0:T(2,128)}, u32[]{:S(2)}) copy-start(s32[2,800,2]{1,2,0:T(2,128)} %param.20) | copy-start | bytes 38404
  4.8 111.2 %copy-start.9 = (bf16[4,768]{1,0:T(4,128)(2,1)S(1)}, bf16[4,768]{1,0:T(4,128)(2,1)}, u32[]{:S(2)}) copy-start(bf16[4,768]{1,0:T(4,128)(2,1)} %param.31) | copy-start | bytes 18436
  303.7 107.7 %copy-start.2 = (f32[2,2,96,768]{3,2,1,0:T(8,128)S(1)}, f32[2,2,96,768]{3,2,1,0:T(8,128)}, u32[]{:S(2)}) copy-start(f32[2,2,96,768]{3,2,1,0:T(8,128)} %get-tuple-element.54) | copy-start | bytes 3538948
  411.4 1.3 copy-start.3
  412.8 1.6 copy-start.4
  412.8 7.7 %copy-start.1 = (f32[2,200,768]{2,1,0:T(8,128)S(1)}, f32[2,200,768]{2,1,0:T(8,128)}, u32[]{:S(2)}) copy-start(f32[2,200,768]{2,1,0:T(8,128)} %get-tuple-element.107) | copy-start | bytes 3686404
  414.3 7.2 %copy-start = (f32[2,200,768]{2,1,0:T(8,128)S(1)}, f32[2,200,768]{2,1,0:T(8,128)}, u32[]{:S(2)}) copy-start(f32[2,200,768]{2,1,0:T(8,128)} %get-tuple-element.108) | copy-start | bytes 3686404

commit v2 on v1

v2 whole, which is shorter than its diff:
```python
import functools
import math

import jax
import jax.numpy as jnp
from jax import lax
from jax.experimental import pallas as pl
from jax.experimental.pallas import tpu as pltpu
from jax.sharding import PartitionSpec as P

HEAD_DIM = 64
NORM_EPS = 1e-06
MASK_FILL = -1000000000.0
MESH = pl.DeviceIdType.MESH
BF = jnp.bfloat16
F32 = jnp.float32
DMA = pltpu.SemaphoreType.DMA

VMEM_LIMIT = 63 << 20


def dot_nn(a, b):
    return lax.dot_general(a, b, (((1,), (0,)), ((), ())), preferred_element_type=F32)


def dot_nt(a, b):
    return lax.dot_general(a, b, (((1,), (1,)), ((), ())), preferred_element_type=F32)


def dot_tn(a, b):
    return lax.dot_general(a, b, (((0,), (0,)), ((), ())), preferred_element_type=F32)


def norm_parts(values):
    row_mean = jnp.mean(values, axis=-1, keepdims=True)
    centred = values - row_mean
    row_var = jnp.mean(centred * centred, axis=-1, keepdims=True)
    inv_std = lax.rsqrt(row_var + NORM_EPS)
    return centred * inv_std, inv_std


def norm_back(scaled, normed, inv_std):
    return inv_std * (
        scaled
        - jnp.mean(scaled, axis=-1, keepdims=True)
        - normed * jnp.mean(scaled * normed, axis=-1, keepdims=True)
    )


def gelu_parts(x):
    z = jnp.abs(x) * (1.0 / math.sqrt(2.0))
    t = 1.0 / (1.0 + 0.3275911 * z)
    expo = jnp.exp(-0.5 * x * x)
    poly = t * (
        0.254829592
        + t * (-0.284496736 + t * (1.421413741 + t * (-1.453152027 + t * 1.061405429)))
    )
    tail = 0.5 * poly * expo
    cdf = jnp.where(x >= 0, 1.0 - tail, tail)
    return x * cdf, cdf + x * (expo * (1.0 / math.sqrt(2.0 * math.pi)))


def remote(src, dst, send, recv, dev):
    return pltpu.make_async_remote_copy(
        src_ref=src, dst_ref=dst, send_sem=send, recv_sem=recv, device_id=dev, device_id_type=MESH
    )


def half_of(count):
    return count // 2


class Net:
    def __init__(self, fsdp):
        self.fsdp = fsdp
        self.half = fsdp // 2
        self.f = f = lax.axis_index("fsdp")
        self.t = t = lax.axis_index("tp")
        self.pf = f + 1 - 2 * lax.rem(f, 2)
        self.t2 = lax.rem(t + 2, 4)
        self.s = t + 1 - 2 * lax.rem(t, 2)
        self.s2 = lax.rem(self.s + 2, 4)
        self.partner = (self.pf, t)
        self.across = (f, self.t2)
        self.sibling = (f, self.s)

    def at(self, base, k):
        return lax.rem(base + 2 * k + self.fsdp, self.fsdp)

    def line(self, k):
        return (self.at(self.f, k), self.t)

    def barrier(self):
        sem = pltpu.get_barrier_semaphore()
        peers = [self.partner, self.across, self.sibling]
        peers += [self.line(k) for k in range(1, self.half)]
        for peer in peers:
            pl.semaphore_signal(sem, inc=1, device_id=peer, device_id_type=MESH)
        pl.semaphore_wait(sem, len(peers))


class Gather:
    def __init__(self, net, block, sems, unit):
        self.net, self.block, self.unit = net, block, unit
        self.ps, self.pr, self.ls, self.lr = sems

    def _pair(self, j, k):
        u = self.unit
        return remote(self.block(j), self.block(j), self.ps.at[u, k], self.pr.at[u, k], self.net.partner)

    def _line(self, j, k):
        u = self.unit
        return remote(self.block(j), self.block(j), self.ls.at[u, k], self.lr.at[u, k], self.net.line(k))

    def send(self, steps):
        for k in steps:
            if k == 0:
                self._pair(self.net.f, 0).start()
            else:
                self._line(self.net.f, k).start()

    def forward(self, steps):
        n = self.net
        for k in steps:
            j = n.at(n.f, -k)
            self._line(j, k).wait_recv()
            self._pair(j, k).start()

    def finish(self):
        n = self.net
        for k in range(n.half):
            self._pair(n.at(n.pf, -k), k).wait_recv()

    def drain(self):
        n = self.net
        for k in range(n.half):
            self._pair(n.f, k).wait_send()
        for k in range(1, n.half):
            self._line(n.f, k).wait_send()


class Reduce:
    def __init__(self, net, block, first, second, sems, unit, fetch=None):
        self.net, self.block, self.first, self.second, self.unit = net, block, first, second, unit
        self.ps, self.pr, self.ls, self.lr = sems
        self.fetch = fetch

    def _pair(self, k):
        n, u = self.net, self.unit
        return remote(
            self.block(n.at(n.pf, k)), self.first(k), self.ps.at[u, k], self.pr.at[u, k], n.partner
        )

    def _line(self, k):
        n, u = self.net, self.unit
        return remote(
            self.block(n.at(n.f, k)), self.second(k), self.ls.at[u, k], self.lr.at[u, k], n.line(k)
        )

    def start(self):
        for k in list(range(1, self.net.half)) + [0]:
            self._pair(k).start()

    def middle(self):
        n = self.net
        for k in range(1, n.half):
            self._pair(k).wait_recv()
            mine = self.block(n.at(n.f, k))
            mine[...] = (mine[...].astype(F32) + self.first(k)[...].astype(F32)).astype(BF)
            self._line(k).start()

    def _load(self, k):
        return pltpu.make_async_copy(self.second(k), self.first(k), self.fetch.at[self.unit, k])

    def collect(self):
        for k in range(1, self.net.half):
            self._line(k).wait_recv()
            self._load(k).start()

    def finish(self):
        n = self.net
        self._pair(0).wait_recv()
        total = self.block(n.f)[...].astype(F32) + self.first(0)[...].astype(F32)
        for k in range(1, n.half):
            if self.fetch is None:
                self._line(k).wait_recv()
                total = total + self.second(k)[...].astype(F32)
            else:
                self._load(k).wait()
                total = total + self.first(k)[...].astype(F32)
        return total

    def drain(self):
        for k in range(self.net.half):
            self._pair(k).wait_send()
        for k in range(1, self.net.half):
            self._line(k).wait_send()


class RowGather:
    def __init__(self, net, block, sems, unit):
        self.net, self.block, self.unit = net, block, unit
        self.ys, self.yr, self.cs, self.cr = sems

    def _y(self, j):
        u = self.unit
        return remote(self.block(j), self.block(j), self.ys.at[u], self.yr.at[u], self.net.across)

    def _c(self, j, k):
        u = self.unit
        return remote(self.block(j), self.block(j), self.cs.at[u, k], self.cr.at[u, k], self.net.sibling)

    def start(self):
        self._y(self.net.t).start()
        self._c(self.net.t, 0).start()

    def forward(self):
        n = self.net
        self._y(n.t2).wait_recv()
        self._c(n.t2, 1).start()

    def finish(self):
        n = self.net
        self._c(n.s, 0).wait_recv()
        self._c(n.s2, 1).wait_recv()

    def drain(self):
        n = self.net
        self._y(n.t).wait_send()
        self._c(n.t, 0).wait_send()
        self._c(n.t2, 1).wait_send()


class RowReduce:
    def __init__(self, net, block, first, second, sems, unit):
        self.net, self.block, self.first, self.second, self.unit = net, block, first, second, unit
        self.ys, self.yr, self.cs, self.cr = sems

    def _c(self, k):
        n, u = self.net, self.unit
        j = n.s2 if k == 0 else n.s
        return remote(self.block(j), self.first(k), self.cs.at[u, k], self.cr.at[u, k], n.sibling)

    def _y(self):
        n, u = self.net, self.unit
        return remote(self.block(n.t2), self.second(), self.ys.at[u], self.yr.at[u], n.across)

    def start(self):
        self._c(0).start()
        self._c(1).start()

    def middle(self, add=None):
        n = self.net
        self._c(0).wait_recv()
        mine = self.block(n.t2)
        if add is None:
            mine[...] = (mine[...].astype(F32) + self.first(0)[...].astype(F32)).astype(BF)
        else:
            add(mine, self.first(0))
        self._y().start()

    def finish(self):
        n = self.net
        self._c(1).wait_recv()
        self._y().wait_recv()
        return (
            self.block(n.t)[...].astype(F32)
            + self.first(1)[...].astype(F32)
            + self.second()[...].astype(F32)
        )

    def drain(self):
        self._c(0).wait_send()
        self._c(1).wait_send()
        self._y().wait_send()


def head_masks(rows, width):
    lane = lax.broadcasted_iota(jnp.int32, (rows, width), 1)
    return [
        (lane >= h * HEAD_DIM) & (lane < (h + 1) * HEAD_DIM) for h in range(width // HEAD_DIM)
    ]


def stack_heads(rows, masks):
    zero = jnp.zeros_like(rows)
    return jnp.concatenate([jnp.where(mask, rows, zero) for mask in masks], axis=0)


def merge_heads(stacked, masks):
    count = masks[0].shape[0]
    total = jnp.where(masks[0], stacked[:count], 0.0)
    for h in range(1, len(masks)):
        total = jnp.where(masks[h], stacked[h * count : (h + 1) * count], total)
    return total


def block_kernel(fsdp, experts, *refs):
    it = iter(refs)
    take = lambda n: [next(it) for _ in range(n)]
    cnt, x_in, dy_in = take(3)
    vectors = take(7)
    qkv_in, mix_in, w1_in, w2_in, b1_in, route_in, prio_in = take(7)
    y_out, gx_out, gq_out, gm_out, g1_out, g2_out = take(6)
    vec_out = take(5)
    router_out, ob_out, hb_out, r2 = take(4)
    rowsb, dyg, rin, qkv, prob, mix, hid, awg, par, parg = take(10)
    wbuf, part, first, second, r1, a1, a2 = take(7)
    hot_s, gts, xs, vs, gas, dps, sid, rp, dmx, hb, ob, b1 = take(12)
    z1, z2, z3, z4, zs = take(5)
    ga = take(4)
    rs = take(4)
    rg = take(4)
    rr = take(4)
    loc, sm_s, sm_r, fetch = take(4)
    net = Net(fsdp)
    f, t = net.f, net.t
    live, width = x_in.shape[1], x_in.shape[2]
    rows = rowsb.shape[1]
    images = rowsb.shape[0] // 2
    full = images * rows
    hw = qkv.shape[3]
    own = width // fsdp
    order = []
    for k in range(1, half_of(fsdp)):
        for step in (k, half_of(fsdp) - k):
            if step not in order:
                order.append(step)
    third = -(-len(order) // 3)
    near, far, last = order[:third], order[third : 2 * third], order[2 * third :]
    no_rows = jnp.zeros((rows - live, width), F32)

    def padded(ref, m):
        return jnp.concatenate([ref[m].astype(F32), no_rows], axis=0)

    slots = hot_s.shape[1]
    ff = wbuf.shape[4]
    wide = 2 * width
    scale = 1.0 / math.sqrt(HEAD_DIM)

    gat_par = Gather(net, lambda j: parg.at[j], ga, 0)
    gat_aw = Gather(net, lambda j: awg.at[j], ga, 1)
    gat = lambda e: Gather(net, lambda j: wbuf.at[e, j], ga, 2 + e)
    red_e = lambda e: Reduce(
        net, lambda j: wbuf.at[e, j], lambda k: r1.at[e, k], lambda k: r2.at[e, k], rs, e, fetch
    )
    red_a = Reduce(net, lambda j: awg.at[j], lambda k: a1.at[k], lambda k: a2.at[k], rs, experts)

    def row_gather(buf, m, unit):
        return RowGather(net, lambda j: buf.at[m * images + j], rg, unit)

    def row_reduce(m, lo, hi, unit):
        return RowReduce(
            net,
            lambda j: part.at[m, j, :, lo:hi],
            lambda k: first.at[m, k, :, lo:hi],
            lambda: second.at[m, :, lo:hi],
            rr,
            unit,
        )

    row_x = [row_gather(rowsb, m, m) for m in range(2)]
    row_dy = [row_gather(dyg, m, 2 + m) for m in range(2)]
    row_n2 = [row_gather(rowsb, m, 4 + m) for m in range(2)]
    row_h = [row_gather(rowsb, m, 6 + m) for m in range(2)]
    red_att = [row_reduce(m, 0, width, m) for m in range(2)]
    red_mid = [row_reduce(m, width, wide + 256, 2 + m) for m in range(2)]
    red_out = [row_reduce(m, 0, width, 4 + m) for m in range(2)]
    red_low = [row_reduce(m, width, wide, 6 + m) for m in range(2)]

    copies = []
    for e in range(experts):
        for i, src in enumerate((w1_in, w2_in)):
            copies.append(pltpu.make_async_copy(src.at[e], wbuf.at[e, f, i], loc.at[2 * e + i]))
    for copy in copies:
        copy.start()
    net.barrier()
    for m in range(2):
        rowsb[m * images + t] = padded(x_in, m).astype(BF)
        row_x[m].start()
    zs[...] = jnp.zeros_like(zs)
    at = 0
    for ref in vectors:
        count = ref.shape[0]
        zs[at : at + count, :own] = ref[...].astype(F32)
        at += count
    parg[f] = zs[0:16, :128].astype(BF)
    gat_par.send([0] + order)
    awg[f] = jnp.concatenate([qkv_in[0], qkv_in[1], qkv_in[2], mix_in[...]], axis=1)
    gat_aw.send([0] + order)
    for m in range(2):
        dyg[m * images + t] = padded(dy_in, m).astype(BF)
    b1[0:experts, :] = b1_in[...].astype(F32)
    gat_par.forward(order)
    row_x[0].forward()
    gat_par.finish()

    place = lax.broadcasted_iota(jnp.int32, (128, width), 0)
    column = lax.broadcasted_iota(jnp.int32, (128, width), 1)
    joined = jnp.zeros((16, width), F32)
    for j in range(fsdp):
        hot = ((column == place + j * own) & (place < own)).astype(BF)
        joined = joined + dot_nn(parg[j], hot)
    par[...] = joined
    gain_one, shift_one = par[0:1, :], par[1:2, :]
    mix_bias, gain_two, shift_two = par[2:3, :], par[3:4, :], par[4:5, :]

    def first_norm(i, carry):
        normed, _ = norm_parts(rowsb[i].astype(F32))
        rin[i] = (normed * gain_one + shift_one).astype(BF)
        return carry

    gat_aw.forward(order)
    for copy in copies:
        copy.wait()
    def send_pair(group):
        for steps in ([0], near, far, last):
            for e in group:
                gat(e).send(steps)

    def forward_pair(group, steps):
        for e in group:
            gat(e).forward(steps)

    send_pair((0, 1))
    row_x[0].finish()
    lax.fori_loop(0, images, first_norm, 0)
    row_x[1].forward()
    for m in range(2):
        row_dy[m].start()
    row_x[1].finish()
    lax.fori_loop(images, 2 * images, first_norm, 0)
    gat_aw.finish()

    def project(m, carry):
        span = pl.ds(m * images, images)
        weights = awg[...].reshape(width, 4 * hw)
        block = rin[span].reshape(full, width)
        for c in range(3):
            made = dot_nn(block, weights[:, c * hw : (c + 1) * hw])
            qkv[c, span] = made.astype(BF).reshape(images, rows, hw)
        return carry

    lax.fori_loop(0, 2, project, 0)
    masks = head_masks(rows, hw)
    key_pos = lax.broadcasted_iota(jnp.int32, (len(masks) * rows, rows), 1)

    def attend(i, carry):
        stacked = stack_heads(qkv[0, i], masks)
        scores = dot_nt(stacked, qkv[1, i]) * scale
        scores = jnp.where(key_pos < cnt[i // images, lax.rem(i, images)], scores, MASK_FILL)
        expo = jnp.exp(scores - jnp.max(scores, axis=-1, keepdims=True))
        probs = (expo / jnp.sum(expo, axis=-1, keepdims=True)).astype(BF)
        prob[i] = probs
        mix[i] = merge_heads(dot_nn(probs, qkv[2, i]), masks).astype(BF)
        return carry

    for op in row_x:
        op.drain()
    out_w = awg[...].reshape(width, 4 * hw)[:, 3 * hw :]
    for m in range(2):
        lax.fori_loop(m * images, (m + 1) * images, attend, 0)
        block = mix[m * images : (m + 1) * images].reshape(full, hw)
        part[m, :, :, :width] = dot_nt(block, out_w).astype(BF).reshape(images, rows, width)
        red_att[m].start()
        if m == 0:
            for op in row_dy:
                op.forward()
            red_att[0].middle()
            forward_pair((0, 1), near)
            send_pair((2, 3))
    red_att[1].middle()

    def second_norm(m, carry):
        hidden = padded(x_in, m) + row_reduce(m, 0, width, m).finish() + mix_bias
        hid[m] = hidden
        normed, _ = norm_parts(hidden)
        rowsb[m * images + t] = (normed * gain_two + shift_two).astype(BF)
        row_gather(rowsb, m, 4 + m).start()
        return carry

    lax.fori_loop(0, 2, second_norm, 0)
    for m in range(2):
        row_n2[m].forward()
        row_dy[m].finish()
        red_att[m].drain()
        part[m] = jnp.zeros_like(part[m])
    forward_pair((0, 1), far)

    hb[...] = jnp.zeros_like(hb)
    ob[...] = jnp.zeros_like(ob)

    def find_slots(m, carry):
        by_image = lambda row, fill: jnp.concatenate(
            sum(
                [
                    [row[:, i * live : (i + 1) * live], jnp.full((1, rows - live), fill, jnp.int32)]
                    for i in range(images)
                ],
                [],
            ),
            axis=1,
        )
        e0, e1 = by_image(route_in[m, 0:1, :], -1), by_image(route_in[m, 1:2, :], -1)
        rank = by_image(prio_in[m], live * images)
        high = rank // 32
        digit = lax.broadcasted_iota(jnp.int32, (16, full), 0)
        digits = jnp.where(digit == 0, high, jnp.where(digit == 1, rank - 32 * high, 0))
        digit = lax.broadcasted_iota(jnp.int32, (16, 128), 0)
        worth = jnp.where(digit == 0, 32, jnp.where(digit == 1, 1, 0))
        column = dot_tn(digits.astype(F32).astype(BF), worth.astype(F32).astype(BF))[:, 0:1]
        lower = (column < rank.astype(F32)).astype(BF)
        kind = lax.broadcasted_iota(jnp.int32, (16, full), 0)
        named = jnp.where(kind < experts, e0, e1) == jnp.where(kind < experts, kind, kind - experts)
        named = jnp.where((kind < 2 * experts) & named, 1.0, 0.0)
        counts = dot_nn(named.astype(BF), lower)
        totals = jnp.sum(named, axis=1, keepdims=True)
        for k in range(2):
            where_slot = jnp.full((1, full), -1.0, F32)
            for e in range(experts):
                c = k * experts + e
                before = counts[c : c + 1, :]
                if k == 1:
                    before = before + totals[e : e + 1, :]
                kept = (named[c : c + 1, :] > 0.5) & (before < slots)
                where_slot = jnp.where(kept, before + e * slots, where_slot)
            sid[m, k : k + 1, :] = where_slot.astype(jnp.int32)
        return carry

    lax.fori_loop(0, 2, find_slots, 0)
    for m in range(2):
        row_n2[m].finish()
        n2m = rowsb[m * images : (m + 1) * images].reshape(full, width)
        logits = dot_nt(par[...].astype(BF), n2m)[5 : 5 + experts, :]
        expo = jnp.exp(logits - jnp.max(logits, axis=0, keepdims=True))
        rp[m, 0:experts, :] = expo / jnp.sum(expo, axis=0, keepdims=True)
        row_n2[m].drain()
    forward_pair((0, 1), last)

    slot_row = lax.broadcasted_iota(jnp.int32, (slots, full), 0)
    lane = lax.broadcasted_iota(jnp.int32, (slots, 128), 1)

    def add_split(mine, other):
        mine[:, :width] = (mine[:, :width].astype(F32) + other[:, :width].astype(F32)).astype(BF)
        pair = [mine[:, width : width + 128].astype(F32), mine[:, width + 128 :].astype(F32)]
        pair += [other[:, width : width + 128].astype(F32), other[:, width + 128 :].astype(F32)]
        value = (pair[0] + pair[2]) + (pair[1] + pair[3])
        high = value.astype(BF)
        mine[:, width : width + 128] = high
        mine[:, width + 128 :] = (value - high.astype(F32)).astype(BF)

    schedule = {
        (0, 1): lambda: forward_pair((2, 3), near),
        (1, 0): lambda: forward_pair((2, 3), far),
        (1, 3): lambda: forward_pair((2,), last),
        (2, 1): lambda: (forward_pair((3,), last), red_e(0).start(), red_e(1).start()),
        (2, 3): lambda: red_e(2).start(),
        (3, 2): lambda: red_mid[0].middle(add_split),
        (3, 3): lambda: (red_e(3).start(), red_mid[1].middle(add_split)),
    }

    def ticks(e, point):
        for (expert_at, point_at), act in schedule.items():
            if point_at == point:

                @pl.when(e == expert_at)
                def _():
                    act()

    def expert(e, carry):
        def dispatch(m, carry):
            hot = (slot_row + e * slots == sid[m, 0:1, :]) | (slot_row + e * slots == sid[m, 1:2, :])
            hot_s[m] = jnp.where(hot, 1.0, 0.0).astype(BF)
            gate = jnp.sum(jnp.where(hot, rp[m, pl.ds(e, 1), :], 0.0), axis=1, keepdims=True)
            gts[m] = jnp.broadcast_to(gate, (slots, 128))
            n2m = rowsb[pl.ds(m * images, images)].reshape(full, width)
            xs[m] = dot_nn(hot_s[m], n2m).astype(BF)
            dym = dyg[pl.ds(m * images, images)].reshape(full, width)
            vals = dot_nn(hot_s[m], dym)
            ob[pl.ds(e, 1), :] += jnp.sum(gate * vals, axis=0, keepdims=True)
            vs[m] = vals.astype(BF)
            return carry

        lax.fori_loop(0, 2, dispatch, 0)
        ticks(e, 0)
        gat(e).finish()


        def hidden_units(m, carry):
            gate = gts[m][:, 0:1]
            d_gate = jnp.zeros((slots, 1), F32)
            for lo in range(0, ff, 256):
                span = slice(lo, lo + 256)
                pre = dot_nn(xs[m], wbuf[e, :, 0, :, span].reshape(width, 256))
                act, slope = gelu_parts(pre + b1[pl.ds(e, 1), span])
                gas[m, :, span] = (gate * act).astype(BF)
                back = dot_nn(vs[m], wbuf[e, :, 1, :, span].reshape(width, 256))
                d_gate = d_gate + jnp.sum(act * back, axis=1, keepdims=True)
                d_pre = gate * slope * back
                hb[pl.ds(e, 1), span] += jnp.sum(d_pre, axis=0, keepdims=True)
                dps[m, :, span] = d_pre.astype(BF)
            high = d_gate.astype(BF)
            low = (d_gate - high.astype(F32)).astype(BF)
            zero = jnp.zeros((slots, 128), BF)
            extra = [
                jnp.where(lane == e, high, jnp.where(lane == 16 + e, jnp.ones_like(zero), zero)),
                jnp.where(lane == e, low, zero),
            ]
            lower, upper = slice(0, fsdp // 2), slice(fsdp // 2, fsdp)
            part_of = lambda i, cut: wbuf[e, cut, i].reshape(width // 2, ff)
            pieces = [
                lambda: dot_nt(gas[m], part_of(1, lower)).astype(BF),
                lambda: dot_nt(gas[m], part_of(1, upper)).astype(BF),
                lambda: dot_nt(dps[m], part_of(0, lower)).astype(BF),
                lambda: dot_nt(dps[m], part_of(0, upper)).astype(BF),
                lambda: jnp.concatenate(extra, axis=1),
            ]
            lo = 0
            for make in pieces:
                piece = make()
                span = slice(lo, lo + piece.shape[1])
                lo = span.stop
                more = dot_tn(hot_s[m], piece).reshape(images, rows, piece.shape[1])
                part[m, :, :, span] = (part[m, :, :, span].astype(F32) + more).astype(BF)

            @pl.when(e == experts - 1)
            def _():
                row_reduce(m, width, wide + 256, 2 + m).start()

            @pl.when(m == 0)
            def _():
                ticks(e, 1)

            return carry

        lax.fori_loop(0, 2, hidden_units, 0)
        ticks(e, 2)
        gat(e).drain()

        two = 2 * slots
        for n in range(2):
            cut = slice(n * (width // 2), (n + 1) * (width // 2))
            blocks = slice(n * fsdp // 2, (n + 1) * fsdp // 2)
            for i, (left, right) in enumerate(((xs, dps), (vs, gas))):
                made = dot_tn(left[:, :, cut].reshape(two, width // 2), right[...].reshape(two, ff))
                wbuf[e, blocks, i] = made.astype(BF).reshape(fsdp // 2, own, ff)
        ticks(e, 3)
        return carry

    lax.fori_loop(0, experts, expert, 0)

    red_e(0).middle()

    zs[...] = jnp.zeros_like(zs)
    lane = lax.broadcasted_iota(jnp.int32, (rows, 128), 1)
    lane16 = lax.broadcasted_iota(jnp.int32, (rows, 16), 1)
    router_lane = (lane16 >= 5) & (lane16 < 5 + experts)

    def router_back(m, carry):
        hidden = hid[m]
        normed, inv = norm_parts(hidden)
        dy = dyg[m * images + t].astype(F32)
        n2 = rowsb[m * images + t]
        logits = jnp.where(router_lane, dot_nt(n2, par[...].astype(BF)), -1e30)
        expo = jnp.exp(logits - jnp.max(logits, axis=1, keepdims=True))
        probs = expo / jnp.sum(expo, axis=1, keepdims=True)
        got = row_reduce(m, width, wide + 256, 2 + m).finish()
        sums = got[:, width : width + 128] + got[:, width + 128 :]
        pcol, qcol, out = [], [], hidden
        for e in range(experts):
            p_e = jnp.sum(jnp.where(lane16 == 5 + e, probs, 0.0), axis=1, keepdims=True)
            kept = 0.25 * jnp.sum(jnp.where(lane == 16 + e, sums, 0.0), axis=1, keepdims=True)
            q_e = jnp.sum(jnp.where(lane == e, sums, 0.0), axis=1, keepdims=True)
            bias = par[5 + experts + e : 6 + experts + e, :]
            q_e = q_e + kept * jnp.sum(dy * bias, axis=1, keepdims=True)
            out = out + (kept * p_e) * bias
            pcol.append(p_e)
            qcol.append(q_e)
        y_out[m] = out[:live]
        mean_q = pcol[0] * qcol[0]
        for e in range(1, experts):
            mean_q = mean_q + pcol[e] * qcol[e]
        mid = got[:, :width]
        for e in range(experts):
            d_logit = (pcol[e] * (qcol[e] - mean_q)).astype(BF).astype(F32)
            mid = mid + d_logit * par[5 + e : 6 + e, :]
            zs[5 + e : 6 + e, :] += jnp.sum(d_logit * n2.astype(F32), axis=0, keepdims=True)
        d_hidden = dy + norm_back(mid * gain_two, normed, inv)
        hid[m] = d_hidden
        rowsb[m * images + t] = d_hidden.astype(BF)
        row_gather(rowsb, m, 6 + m).start()
        zs[2:3, :] += jnp.sum(d_hidden, axis=0, keepdims=True)
        zs[3:4, :] += jnp.sum(mid * normed, axis=0, keepdims=True)
        zs[4:5, :] += jnp.sum(mid, axis=0, keepdims=True)
        return carry

    lax.fori_loop(0, 2, router_back, 0)
    zs[5 + experts : 5 + 2 * experts, :] = 0.25 * ob[0:experts, :]
    zs[16 : 16 + experts, :] = hb[0:experts, :]
    for m in range(2):
        row_h[m].forward()
        red_mid[m].drain()
    red_e(1).middle()

    def attend_back(i, carry):
        stacked_d = stack_heads(dmx[i], masks)
        stacked_q = stack_heads(qkv[0, i], masks)
        probs_low = prob[i]
        probs = probs_low.astype(F32)
        d_prob = dot_nt(stacked_d, qkv[2, i])
        d_score = probs * (d_prob - jnp.sum(probs * d_prob, axis=-1, keepdims=True))
        d_score = d_score.astype(BF)
        qkv[0, i] = (merge_heads(dot_nn(d_score, qkv[1, i]), masks) * scale).astype(BF)
        qkv[1, i] = (dot_tn(d_score, stacked_q) * scale).astype(BF)
        qkv[2, i] = dot_tn(probs_low, stacked_d).astype(BF)
        return carry

    for m in range(2):
        row_h[m].finish()
        red_out[m].start()
        span = slice(m * images, (m + 1) * images)
        block = rowsb[span].reshape(full, width)
        weights = awg[...].reshape(width, 4 * hw)
        dmx[span] = dot_nn(block, weights[:, 3 * hw :]).astype(BF).reshape(images, rows, hw)
        lax.fori_loop(m * images, (m + 1) * images, attend_back, 0)
        for n in range(2):
            cut = slice(n * fsdp // 2, (n + 1) * fsdp // 2)
            weights = awg[cut].reshape(width // 2, 4 * hw)
            low = jnp.zeros((full, width // 2), F32)
            for c in range(3):
                low = low + dot_nt(qkv[c, span].reshape(full, hw), weights[:, c * hw : (c + 1) * hw])
            here = slice(n * (width // 2), (n + 1) * (width // 2))
            zs[1:2, here] += jnp.sum(low, axis=0, keepdims=True)
            normed = rin[span, :, here].astype(F32).reshape(full, width // 2)
            zs[0:1, here] += jnp.sum(low * normed, axis=0, keepdims=True)
            at = width + n * (width // 2)
            part[m, :, :, at : at + width // 2] = low.astype(BF).reshape(images, rows, width // 2)
        red_low[m].start()
        red_low[m].middle()
        red_out[m].middle()

    gat_aw.drain()

    def att_grads(n, carry):
        cut = pl.ds(pl.multiple_of(n * (width // 2), 128), width // 2)
        flat_in = rin[:, :, cut].reshape(2 * full, width // 2)
        made = [dot_tn(flat_in, qkv[c].reshape(2 * full, hw)) for c in range(3)]
        flat_h = rowsb[:, :, cut].reshape(2 * full, width // 2)
        made.append(dot_tn(flat_h, mix[...].reshape(2 * full, hw)))
        joined = jnp.concatenate(made, axis=1).astype(BF)
        awg[pl.ds(n * (fsdp // 2), fsdp // 2)] = joined.reshape(fsdp // 2, own, 4 * hw)
        return carry

    zs[0:1, :] = (zs[0:1, :] - shift_one * zs[1:2, :]) / gain_one

    hops = [(z1, 16, net.sibling), (z2, 16, net.across), (z3, 24, net.partner)]

    def hop(i):
        buf, count, dev = hops[i]
        return remote(zs.at[0:count], buf, sm_s.at[i], sm_r.at[i], dev)

    def hop_end(i):
        buf, count, dev = hops[i]
        hop(i).wait()
        zs[0:count] = zs[0:count] + buf[...]

    hop(0).start()
    lax.fori_loop(0, 2, att_grads, 0)
    red_a.start()
    red_e(2).middle()
    hop_end(0)
    hop(1).start()

    def first_back(m, carry):
        low = row_reduce(m, width, wide, 6 + m).finish()
        normed, inv = norm_parts(padded(x_in, m))
        gx_out[m] = (hid[m] + norm_back(low * gain_one, normed, inv))[:live]
        return carry

    lax.fori_loop(0, 2, first_back, 0)
    hop_end(1)
    hop(2).start()
    for m in range(2):
        y_out[m] += red_out[m].finish()[:live]
    hop_end(2)
    for k in range(1, net.half):
        remote(zs, z4.at[k], sm_s.at[2 + k], sm_r.at[2 + k], net.line(k)).start()
    red_e(3).middle()
    red_a.middle()
    for e in range(experts - 1):
        red_e(e).collect()
    outs = []
    red_e(experts - 1).collect()
    for e in range(experts):
        both = red_e(e).finish()
        for i, dst in enumerate((g1_out, g2_out)):
            if e > 1:
                outs[2 * e - 4 + i].wait()
            stage = hid.at[e % 2, i * own : (i + 1) * own]
            stage[...] = both[i]
            outs.append(pltpu.make_async_copy(stage, dst.at[e], loc.at[2 * e + i]))
            outs[-1].start()
    made = red_a.finish()
    for c in range(3):
        gq_out[c] = made[:, c * hw : (c + 1) * hw]
    gm_out[...] = made[:, 3 * hw :]
    sums = zs[...]
    for k in range(1, net.half):
        remote(zs, z4.at[k], sm_s.at[2 + k], sm_r.at[2 + k], net.line(k)).wait()
        sums = sums + z4[k]
    hb_out[...] = sums[16 : 16 + experts]
    mine = pltpu.roll(sums, lax.rem(width - own * f, width), 1)[:, :own]
    for i in range(5):
        vec_out[i][...] = mine[i : i + 1]
    router_out[...] = mine[5 : 5 + experts]
    ob_out[...] = mine[5 + experts : 5 + 2 * experts]
    for copy in outs[-4:]:
        copy.wait()
    for op in [red_e(e) for e in range(experts)] + [red_a, gat_par] + row_dy + row_h + red_out + red_low:
        op.drain()


def vmem(shape, dtype=BF):
    return pltpu.VMEM(shape, dtype)


def spec(space):
    return pl.BlockSpec(memory_space=space)


V = pltpu.VMEM
H = pltpu.HBM


def pair_sems(units, half):
    return [DMA((units, half)) for _ in range(4)]


def row_sems(units):
    return [DMA((units,)), DMA((units,)), DMA((units, 2)), DMA((units, 2))]


def per_device(
    patch_embeddings,
    upstream_gradient,
    picture_valid_count,
    assigned_specialists,
    filling_sequence_place,
    leading_scale_factor,
    leading_offset_vector,
    query_value_matrix,
    mixing_projection_matrix,
    mixing_offset_vector,
    central_scale_factor,
    central_offset_vector,
    gating_projection,
    specialist_widen_matrix,
    specialist_inner_offset,
    specialist_contract_matrix,
    specialist_final_offset,
):
    fsdp = lax.axis_size("fsdp")
    half = fsdp // 2
    tp = lax.axis_size("tp")
    own_rows, width = patch_embeddings.shape[1:]
    rows = -(-own_rows // 16) * 16
    images = tp
    full = images * rows
    own = leading_scale_factor.shape[0]
    hw = query_value_matrix.shape[2]
    heads = hw // HEAD_DIM
    experts, _, ff = specialist_widen_matrix.shape
    slots = 2 * own_rows * tp // experts
    f_index = lax.axis_index("fsdp")

    row = lambda v: v.reshape(1, own)
    vectors = [
        row(leading_scale_factor),
        row(leading_offset_vector),
        row(mixing_offset_vector),
        row(central_scale_factor),
        row(central_offset_vector),
        gating_projection.T,
        specialist_final_offset,
    ]
    w1 = specialist_widen_matrix
    w2 = specialist_contract_matrix.transpose(0, 2, 1)
    sds = jax.ShapeDtypeStruct
    wide = 2 * width + 256
    outs = pl.pallas_call(
        functools.partial(block_kernel, fsdp, experts),
        out_shape=[
            sds((2, own_rows, width), F32),
            sds((2, own_rows, width), F32),
            sds((3, own, hw), F32),
            sds((own, hw), F32),
            sds((experts, own, ff), F32),
            sds((experts, own, ff), F32),
        ]
        + [sds((1, own), F32)] * 5
        + [
            sds((experts, own), F32),
            sds((experts, own), F32),
            sds((experts, ff), F32),
            sds((experts, half, 2, own, ff), BF),
        ],
        in_specs=[spec(pltpu.SMEM)] + [spec(V)] * 11 + [spec(H)] * 2 + [spec(V)] * 3,
        out_specs=[spec(V)] * 4 + [spec(H)] * 2 + [spec(V)] * 8 + [spec(H)],
        scratch_shapes=[
            vmem((2 * images, rows, width)),
            vmem((2 * images, rows, width)),
            vmem((2 * images, rows, width)),
            vmem((3, 2 * images, rows, hw)),
            vmem((2 * images, heads * rows, rows)),
            vmem((2 * images, rows, hw)),
            vmem((2, rows, width), F32),
            vmem((fsdp, own, 4 * hw)),
            vmem((16, width), F32),
            vmem((fsdp, 16, 128)),
            vmem((experts, fsdp, 2, own, ff)),
            vmem((2, images, rows, wide)),
            vmem((2, 2, rows, wide)),
            vmem((2, rows, wide)),
            vmem((experts, half, 2, own, ff)),
            vmem((half, own, 4 * hw)),
            vmem((half, own, 4 * hw)),
            vmem((2, slots, full)),
            vmem((2, slots, 128), F32),
            vmem((2, slots, width)),
            vmem((2, slots, width)),
            vmem((2, slots, ff)),
            vmem((2, slots, ff)),
            vmem((2, 8, full), jnp.int32),
            vmem((2, 8, full), F32),
            vmem((2 * images, rows, hw)),
            vmem((8, ff), F32),
            vmem((8, width), F32),
            vmem((8, ff), F32),
            vmem((16, width), F32),
            vmem((16, width), F32),
            vmem((24, width), F32),
            vmem((half, 24, width), F32),
            vmem((24, width), F32),
        ]
        + pair_sems(2 + experts, half)
        + pair_sems(1 + experts, half)
        + row_sems(8)
        + row_sems(8)
        + [DMA((2 * experts + 2,)), DMA((2 + half,)), DMA((2 + half,)), DMA((experts, half))],
        compiler_params=pltpu.CompilerParams(
            collective_id=1, has_side_effects=True, vmem_limit_bytes=VMEM_LIMIT
        ),
        name="block",
    )(
        picture_valid_count,
        patch_embeddings,
        upstream_gradient,
        *vectors,
        query_value_matrix.transpose(1, 0, 2),
        mixing_projection_matrix.T,
        w1,
        w2,
        specialist_inner_offset,
        assigned_specialists.transpose(0, 2, 1),
        filling_sequence_place,
    )
    flat = [v.reshape(own) for v in outs[6:11]]
    return (
        outs[0],
        outs[1],
        flat[0],
        flat[1],
        outs[2].transpose(1, 0, 2),
        outs[3].T,
        flat[2],
        flat[3],
        flat[4],
        outs[11].T,
        outs[4],
        outs[13],
        outs[5].transpose(0, 2, 1),
        outs[12],
    )


def solution(mesh):
    placed = (
        P(None, ("fsdp", "tp"), None),
        P(None, ("fsdp", "tp"), None),
        P(None, "fsdp"),
        P(None, "fsdp", None),
        P(None, "fsdp", None),
        P("fsdp"),
        P("fsdp"),
        P("fsdp", None, "tp"),
        P("tp", "fsdp"),
        P("fsdp"),
        P("fsdp"),
        P("fsdp"),
        P("fsdp", None),
        P(None, "fsdp", "tp"),
        P(None, "tp"),
        P(None, "tp", "fsdp"),
        P(None, "fsdp"),
    )
    return jax.shard_map(
        per_device,
        mesh=mesh,
        in_specs=placed,
        out_specs=(
            P(None, ("fsdp", "tp"), None),
            P(None, ("fsdp", "tp"), None),
            P("fsdp"),
            P("fsdp"),
            P("fsdp", None, "tp"),
            P("tp", "fsdp"),
            P("fsdp"),
            P("fsdp"),
            P("fsdp"),
            P("fsdp", None),
            P(None, "fsdp", "tp"),
            P(None, "tp"),
            P(None, "tp", "fsdp"),
            P(None, "fsdp"),
        ),
        check_vma=False,
    )
```

time: 430 us -> 319 us (0.74); the launches traced: 423 us -> 317 us
  Pallas kernels: 401 us -> 303 us
  local copies, waits for them, and re-layouts: 18.6 us -> 13.8 us
    pallas_call x3 -> x1, Pallas kernels: 401 us -> 303 us  [per_device(): pl.pallas_call(functools.partial(block_kernel, fsdp, experts), out_shape=...]
    unnamed x43 -> x39, local copies, waits for them, and re-layouts: 5.25 us -> 13.8 us
    pad x5 -> x0, local copies, waits for them, and re-layouts: 4.63 us -> none  [the longest x1 2.05 us: per_device(): x_own = jnp.pad(patch_embeddings, pad_rows)]
where the time goes in v2:
time: 319 us; the launch traced here: 317 us
  Pallas kernels  303 us (95%)
  local copies, waits for them, and re-layouts  13.8 us (4%)
    pallas_call x1, Pallas kernels, per_device(): pl.pallas_call(functools.partial(block_kernel, fsdp, experts), out_shape=...  303 us
    unnamed x39, local copies, waits for them, and re-layouts  13.8 us

profile of v2, /device:TPU:0, one launch (start us, length us, event | category | flops | bytes accessed | tf_op | source)
XLA Modules:
  0.0 317.2 jit_solution(14239459579001294076)
XLA Ops:
  0.6 1.5 copy.31
  2.2 302.7 %block.1 = (f32[2,200,768]{2,1,0:T(8,128)}, f32[2,200,768]{2,1,0:T(8,128)}, f32[3,96,192]{2,1,0:T(8,128)}, f32[96,192]{1,0:T(8,128)}, f32[4,96,768]{2,1,0:T(8,12...) custom-call(s32[2,4]{1,0:T(2,128)} %refs_0_.1, ...), custom_call_target="tpu_custom_call" | custom-call | tf_op jit(solution)/shard_map/block/pallas_call | solution.py:890
  304.8 1.6 copy.32
  306.5 0.0 copy-start
  306.5 2.5 copy.46
  309.0 0.0 copy-done
  309.0 0.0 copy-start.11
  309.0 0.0 copy-start.10
  309.0 0.0 copy-start.3
  309.0 0.0 copy-start.9
  309.0 0.0 copy-start.8
  309.0 0.0 copy-start.7
  309.0 0.0 copy-start.6
  309.0 0.0 copy-start.2
  309.0 1.0 copy.47
  310.1 0.0 copy-done.11
  310.1 0.5 copy.48
  310.6 0.0 copy-done.10
  310.6 0.5 copy.49
  311.1 0.0 copy-done.3
  311.1 0.7 copy.50
  311.8 0.0 copy-done.9
  311.8 0.0 copy-start.4
  311.8 0.0 copy-start.1
  311.8 0.5 copy.51
  312.3 0.0 copy-done.8
  312.3 0.5 copy.52
  312.8 0.0 copy-done.7
  312.8 0.5 copy.53
  313.4 0.0 copy-done.6
  313.4 0.6 copy.54
  313.9 0.0 copy-done.2
  313.9 1.0 copy.55
  315.0 0.0 copy-done.4
  315.0 0.0 copy-start.5
  315.0 0.6 copy.56
  315.6 0.0 copy-done.1
  315.6 1.0 copy.57
  316.6 0.0 copy-done.5
  316.6 0.6 copy.58
Async XLA Ops:
  306.5 2.5 copy-start
  309.0 1.1 copy-start.11
  309.0 1.6 copy-start.10
  309.0 2.1 copy-start.3
  309.0 2.8 copy-start.9
  309.0 3.3 %copy-start.8 = (f32[1,96]{1,0:T(1,128)S(1)}, f32[1,96]{1,0:T(1,128)}, u32[]{:S(2)}) copy-start(f32[1,96]{1,0:T(1,128)} %get-tuple-element.35) | copy-start | bytes 1156
  309.0 3.8 %copy-start.7 = (f32[1,96]{1,0:T(1,128)S(1)}, f32[1,96]{1,0:T(1,128)}, u32[]{:S(2)}) copy-start(f32[1,96]{1,0:T(1,128)} %get-tuple-element.36) | copy-start | bytes 1156
  309.0 4.3 %copy-start.6 = (f32[4,96]{1,0:T(4,128)S(1)}, f32[4,96]{1,0:T(4,128)}, u32[]{:S(2)}) copy-start(f32[4,96]{1,0:T(4,128)} %get-tuple-element.37) | copy-start | bytes 4612
  309.0 4.9 %copy-start.2 = (f32[4,96,768]{2,1,0:T(8,128)S(1)}, f32[4,96,768]{2,1,0:T(8,128)}, u32[]{:S(2)}) copy-start(f32[4,96,768]{2,1,0:T(8,128)} %get-tuple-element.80) | copy-start | bytes 3538948
  311.8 3.1 copy-start.4
  311.8 3.7 %copy-start.1 = (f32[4,96,768]{2,1,0:T(8,128)S(1)}, f32[4,96,768]{2,1,0:T(8,128)}, u32[]{:S(2)}) copy-start(f32[4,96,768]{2,1,0:T(8,128)} %get-tuple-element.40) | copy-start | bytes 3538948
  315.0 1.6 copy-start.5

commit v3 on v2

--- a/solution.py
+++ b/solution.py
@@ -161,9 +161,9 @@
         for k in list(range(1, self.net.half)) + [0]:
             self._pair(k).start()
 
-    def middle(self):
+    def middle(self, steps):
         n = self.net
-        for k in range(1, n.half):
+        for k in steps:
             self._pair(k).wait_recv()
             mine = self.block(n.at(n.f, k))
             mine[...] = (mine[...].astype(F32) + self.first(k)[...].astype(F32)).astype(BF)
@@ -302,8 +302,7 @@
     vectors = take(7)
     qkv_in, mix_in, w1_in, w2_in, b1_in, route_in, prio_in = take(7)
     y_out, gx_out, gq_out, gm_out, g1_out, g2_out = take(6)
-    vec_out = take(5)
-    router_out, ob_out, hb_out, r2 = take(4)
+    small_out, r2 = take(2)
     rowsb, dyg, rin, qkv, prob, mix, hid, awg, par, parg = take(10)
     wbuf, part, first, second, r1, a1, a2 = take(7)
     hot_s, gts, xs, vs, gas, dps, sid, rp, dmx, hb, ob, b1 = take(12)
@@ -327,6 +326,8 @@
             if step not in order:
                 order.append(step)
     third = -(-len(order) // 3)
+    steps = list(range(1, half_of(fsdp)))
+    low_steps, mid_steps, high_steps = steps[:third], steps[third : 2 * third], steps[2 * third :]
     near, far, last = order[:third], order[third : 2 * third], order[2 * third :]
     no_rows = jnp.zeros((rows - live, width), F32)
 
@@ -386,7 +387,9 @@
         at += count
     parg[f] = zs[0:16, :128].astype(BF)
     gat_par.send([0] + order)
-    awg[f] = jnp.concatenate([qkv_in[0], qkv_in[1], qkv_in[2], mix_in[...]], axis=1)
+    same = lax.broadcasted_iota(jnp.int32, (hw, hw), 0) == lax.broadcasted_iota(jnp.int32, (hw, hw), 1)
+    turned = dot_tn(mix_in[...], same.astype(BF)).astype(BF)
+    awg[f] = jnp.concatenate([qkv_in[0], qkv_in[1], qkv_in[2], turned], axis=1)
     gat_aw.send([0] + order)
     for m in range(2):
         dyg[m * images + t] = padded(dy_in, m).astype(BF)
@@ -480,12 +483,12 @@
         return carry
 
     lax.fori_loop(0, 2, second_norm, 0)
+    forward_pair((0, 1), far)
     for m in range(2):
         row_n2[m].forward()
         row_dy[m].finish()
         red_att[m].drain()
         part[m] = jnp.zeros_like(part[m])
-    forward_pair((0, 1), far)
 
     hb[...] = jnp.zeros_like(hb)
     ob[...] = jnp.zeros_like(ob)
@@ -552,10 +555,11 @@
     schedule = {
         (0, 1): lambda: forward_pair((2, 3), near),
         (1, 0): lambda: forward_pair((2, 3), far),
-        (1, 3): lambda: forward_pair((2,), last),
-        (2, 1): lambda: (forward_pair((3,), last), red_e(0).start(), red_e(1).start()),
+        (1, 2): lambda: forward_pair((2,), last),
+        (2, 0): lambda: (forward_pair((3,), last), red_e(0).start(), red_e(1).start()),
         (2, 3): lambda: red_e(2).start(),
-        (3, 2): lambda: red_mid[0].middle(add_split),
+        (3, 1): lambda: red_e(0).middle(low_steps),
+        (3, 2): lambda: (red_mid[0].middle(add_split), red_e(0).middle(mid_steps)),
         (3, 3): lambda: (red_e(3).start(), red_mid[1].middle(add_split)),
     }
 
@@ -649,7 +653,8 @@
 
     lax.fori_loop(0, experts, expert, 0)
 
-    red_e(0).middle()
+    red_e(0).middle(high_steps)
+    red_e(1).middle(low_steps + mid_steps)
 
     zs[...] = jnp.zeros_like(zs)
     lane = lax.broadcasted_iota(jnp.int32, (rows, 128), 1)
@@ -689,6 +694,11 @@
         hid[m] = d_hidden
         rowsb[m * images + t] = d_hidden.astype(BF)
         row_gather(rowsb, m, 6 + m).start()
+
+        @pl.when(m == 0)
+        def _():
+            red_e(1).middle(high_steps)
+
         zs[2:3, :] += jnp.sum(d_hidden, axis=0, keepdims=True)
         zs[3:4, :] += jnp.sum(mid * normed, axis=0, keepdims=True)
         zs[4:5, :] += jnp.sum(mid, axis=0, keepdims=True)
@@ -700,7 +710,6 @@
     for m in range(2):
         row_h[m].forward()
         red_mid[m].drain()
-    red_e(1).middle()
 
     def attend_back(i, carry):
         stacked_d = stack_heads(dmx[i], masks)
@@ -717,7 +726,6 @@
 
     for m in range(2):
         row_h[m].finish()
-        red_out[m].start()
         span = slice(m * images, (m + 1) * images)
         block = rowsb[span].reshape(full, width)
         weights = awg[...].reshape(width, 4 * hw)
@@ -737,7 +745,7 @@
             part[m, :, :, at : at + width // 2] = low.astype(BF).reshape(images, rows, width // 2)
         red_low[m].start()
         red_low[m].middle()
-        red_out[m].middle()
+        red_e(2).middle((low_steps + mid_steps, high_steps)[m])
 
     gat_aw.drain()
 
@@ -766,10 +774,10 @@
 
     hop(0).start()
     lax.fori_loop(0, 2, att_grads, 0)
-    red_a.start()
-    red_e(2).middle()
     hop_end(0)
     hop(1).start()
+    for m in range(2):
+        red_out[m].start()
 
     def first_back(m, carry):
         low = row_reduce(m, width, wide, 6 + m).finish()
@@ -780,18 +788,12 @@
     lax.fori_loop(0, 2, first_back, 0)
     hop_end(1)
     hop(2).start()
+    red_a.start()
     for m in range(2):
-        y_out[m] += red_out[m].finish()[:live]
-    hop_end(2)
-    for k in range(1, net.half):
-        remote(zs, z4.at[k], sm_s.at[2 + k], sm_r.at[2 + k], net.line(k)).start()
-    red_e(3).middle()
-    red_a.middle()
-    for e in range(experts - 1):
-        red_e(e).collect()
+        red_out[m].middle()
     outs = []
-    red_e(experts - 1).collect()
-    for e in range(experts):
+
+    def expert_out(e):
         both = red_e(e).finish()
         for i, dst in enumerate((g1_out, g2_out)):
             if e > 1:
@@ -800,6 +802,22 @@
             stage[...] = both[i]
             outs.append(pltpu.make_async_copy(stage, dst.at[e], loc.at[2 * e + i]))
             outs[-1].start()
+
+    red_e(0).collect()
+    red_e(1).collect()
+    expert_out(0)
+    expert_out(1)
+    red_e(3).middle(steps)
+    hop_end(2)
+    for k in range(1, net.half):
+        remote(zs, z4.at[k], sm_s.at[2 + k], sm_r.at[2 + k], net.line(k)).start()
+    for m in range(2):
+        y_out[m] += red_out[m].finish()[:live]
+    red_e(2).collect()
+    expert_out(2)
+    red_a.middle(steps)
+    red_e(3).collect()
+    expert_out(3)
     made = red_a.finish()
     for c in range(3):
         gq_out[c] = made[:, c * hw : (c + 1) * hw]
@@ -808,16 +826,41 @@
     for k in range(1, net.half):
         remote(zs, z4.at[k], sm_s.at[2 + k], sm_r.at[2 + k], net.line(k)).wait()
         sums = sums + z4[k]
+    small_out[...] = sums
+    for copy in outs[-4:]:
+        copy.wait()
+    for op in [red_e(e) for e in range(experts)] + [red_a, gat_par] + row_dy + row_h + red_out + red_low:
+        op.drain()
+
+
+def finish_kernel(own, experts, *refs):
+    it = iter(refs)
+    take = lambda n: [next(it) for _ in range(n)]
+    small, gm = take(2)
+    large = take(5)
+    vec_out = take(5)
+    router_out, ob_out, hb_out, gm_out = take(4)
+    large_out = take(5)
+    held = take(5)
+    (sem,) = take(1)
+    loads = [pltpu.make_async_copy(large[i], held[i], sem.at[0, i]) for i in range(5)]
+    stores = [pltpu.make_async_copy(held[i], large_out[i], sem.at[1, i]) for i in range(5)]
+    for load in loads:
+        load.start()
+    for load, store in zip(loads, stores):
+        load.wait()
+        store.start()
+    sums = small[...]
+    width = sums.shape[1]
     hb_out[...] = sums[16 : 16 + experts]
-    mine = pltpu.roll(sums, lax.rem(width - own * f, width), 1)[:, :own]
+    mine = pltpu.roll(sums, lax.rem(width - own * lax.axis_index("fsdp"), width), 1)[:, :own]
     for i in range(5):
         vec_out[i][...] = mine[i : i + 1]
     router_out[...] = mine[5 : 5 + experts]
     ob_out[...] = mine[5 + experts : 5 + 2 * experts]
-    for copy in outs[-4:]:
-        copy.wait()
-    for op in [red_e(e) for e in range(experts)] + [red_a, gat_par] + row_dy + row_h + red_out + red_low:
-        op.drain()
+    gm_out[...] = gm[...].T
+    for store in stores:
+        store.wait()
 
 
 def vmem(shape, dtype=BF):
@@ -897,15 +940,12 @@
             sds((experts, own, ff), F32),
             sds((experts, own, ff), F32),
         ]
-        + [sds((1, own), F32)] * 5
         + [
-            sds((experts, own), F32),
-            sds((experts, own), F32),
-            sds((experts, ff), F32),
+            sds((24, width), F32),
             sds((experts, half, 2, own, ff), BF),
         ],
         in_specs=[spec(pltpu.SMEM)] + [spec(V)] * 11 + [spec(H)] * 2 + [spec(V)] * 3,
-        out_specs=[spec(V)] * 4 + [spec(H)] * 2 + [spec(V)] * 8 + [spec(H)],
+        out_specs=[spec(V)] * 4 + [spec(H)] * 2 + [spec(V), spec(H)],
         scratch_shapes=[
             vmem((2 * images, rows, width)),
             vmem((2 * images, rows, width)),
@@ -957,29 +997,48 @@
         upstream_gradient,
         *vectors,
         query_value_matrix.transpose(1, 0, 2),
-        mixing_projection_matrix.T,
+        mixing_projection_matrix,
         w1,
         w2,
         specialist_inner_offset,
         assigned_specialists.transpose(0, 2, 1),
         filling_sequence_place,
     )
-    flat = [v.reshape(own) for v in outs[6:11]]
+    y_out, gx_out, gq, gm, g1, g2, small = outs[:7]
+    large = [y_out, gx_out, gq, g1, g2]
+    outs = pl.pallas_call(
+        functools.partial(finish_kernel, own, experts),
+        out_shape=[sds((1, own), F32)] * 5
+        + [
+            sds((experts, own), F32),
+            sds((experts, own), F32),
+            sds((experts, ff), F32),
+            sds((hw, own), F32),
+        ]
+        + [sds(v.shape, F32) for v in large],
+        in_specs=[spec(V)] * 2 + [spec(H)] * 5,
+        out_specs=[spec(V)] * 9 + [spec(H)] * 5,
+        scratch_shapes=[vmem(v.shape, F32) for v in large] + [DMA((2, 5))],
+        compiler_params=pltpu.CompilerParams(vmem_limit_bytes=VMEM_LIMIT),
+        name="finish",
+    )(small, gm, *large)
+    flat = [v.reshape(own) for v in outs[:5]]
+    router, ob, hb, gm, y_out, gx_out, gq, g1, g2 = outs[5:]
     return (
-        outs[0],
-        outs[1],
+        y_out,
+        gx_out,
         flat[0],
         flat[1],
-        outs[2].transpose(1, 0, 2),
-        outs[3].T,
+        gq.transpose(1, 0, 2),
+        gm,
         flat[2],
         flat[3],
         flat[4],
-        outs[11].T,
-        outs[4],
-        outs[13],
-        outs[5].transpose(0, 2, 1),
-        outs[12],
+        router.T,
+        g1,
+        hb,
+        g2.transpose(0, 2, 1),
+        ob,
     )
 
 

time: 319 us -> 283 us (0.89)
  Pallas kernels: 303 us -> 281 us
  local copies, waits for them, and re-layouts: 13.8 us -> 0 us
    pallas_call x1, Pallas kernels: 303 us -> 276 us  [per_device(): pl.pallas_call(functools.partial(block_kernel, fsdp, experts), out_shape=...]
    unnamed x39 -> x0, local copies, waits for them, and re-layouts: 13.8 us -> none
    pallas_call x0 -> x1, Pallas kernels: none -> 5.74 us  [per_device(): pl.pallas_call(functools.partial(finish_kernel, own, experts), out_shape=...]
where the time goes in v3:
time: 283 us; the launch traced here: 282 us
  Pallas kernels  281 us (99%)
    pallas_call x1, Pallas kernels, per_device(): pl.pallas_call(functools.partial(block_kernel, fsdp, experts), out_shape=...  276 us
    pallas_call x1, Pallas kernels, per_device(): pl.pallas_call(functools.partial(finish_kernel, own, experts), out_shape=...  5.74 us

profile of v3, /device:TPU:0, one launch (start us, length us, event | category | flops | bytes accessed | tf_op | source)
XLA Modules:
  0.0 282.3 jit_solution(11701036485155299688)
XLA Ops:
  0.7 275.7 %block.1 = (f32[2,200,768]{2,1,0:T(8,128)}, f32[2,200,768]{2,1,0:T(8,128)}, f32[3,96,192]{2,1,0:T(8,128)}, f32[96,192]{1,0:T(8,128)}, f32[4,96,768]{2,1,0:T(8,12...) custom-call(s32[2,4]{1,0:T(2,128)} %refs_0_.1, bf16[2,200,768]{2,1,0:T(8,128)(2,1)} %refs_1_.1, ...), custom_call_target="tpu_custom_call" | custom-call | tf_op jit(solution)/shard_map/block/pallas_call | solution.py:933
  276.4 5.7 %finish.1 = (f32[1,96]{1,0:T(1,128)}, f32[1,96]{1,0:T(1,128)}, f32[1,96]{1,0:T(1,128)}, f32[1,96]{1,0:T(1,128)}, f32[1,96]{1,0:T(1,128)}, /*index=5*/f32[4,96]{1...) custom-call(f32[24,768]{1,0:T(8,128)} %get-tuple-element.35.refs_0_,, ...), custom_call_target="tpu_custom_call" | custom-call | tf_op jit(solution)/shard_map/finish/pallas_call | solution.py:1009

commit v4 on v3

--- a/solution.py
+++ b/solution.py
@@ -90,13 +90,14 @@
     def line(self, k):
         return (self.at(self.f, k), self.t)
 
-    def barrier(self):
-        sem = pltpu.get_barrier_semaphore()
+    def arrive(self):
         peers = [self.partner, self.across, self.sibling]
         peers += [self.line(k) for k in range(1, self.half)]
         for peer in peers:
-            pl.semaphore_signal(sem, inc=1, device_id=peer, device_id_type=MESH)
-        pl.semaphore_wait(sem, len(peers))
+            pl.semaphore_signal(
+                pltpu.get_barrier_semaphore(), inc=1, device_id=peer, device_id_type=MESH
+            )
+        return len(peers)
 
 
 class Gather:
@@ -369,16 +370,13 @@
     red_out = [row_reduce(m, 0, width, 4 + m) for m in range(2)]
     red_low = [row_reduce(m, width, wide, 6 + m) for m in range(2)]
 
+    arrived = net.arrive()
     copies = []
     for e in range(experts):
         for i, src in enumerate((w1_in, w2_in)):
             copies.append(pltpu.make_async_copy(src.at[e], wbuf.at[e, f, i], loc.at[2 * e + i]))
     for copy in copies:
         copy.start()
-    net.barrier()
-    for m in range(2):
-        rowsb[m * images + t] = padded(x_in, m).astype(BF)
-        row_x[m].start()
     zs[...] = jnp.zeros_like(zs)
     at = 0
     for ref in vectors:
@@ -386,11 +384,16 @@
         zs[at : at + count, :own] = ref[...].astype(F32)
         at += count
     parg[f] = zs[0:16, :128].astype(BF)
-    gat_par.send([0] + order)
     same = lax.broadcasted_iota(jnp.int32, (hw, hw), 0) == lax.broadcasted_iota(jnp.int32, (hw, hw), 1)
     turned = dot_tn(mix_in[...], same.astype(BF)).astype(BF)
     awg[f] = jnp.concatenate([qkv_in[0], qkv_in[1], qkv_in[2], turned], axis=1)
+    for m in range(2):
+        rowsb[m * images + t] = padded(x_in, m).astype(BF)
+    pl.semaphore_wait(pltpu.get_barrier_semaphore(), arrived)
+    gat_par.send([0] + order)
+    row_x[0].start()
     gat_aw.send([0] + order)
+    row_x[1].start()
     for m in range(2):
         dyg[m * images + t] = padded(dy_in, m).astype(BF)
     b1[0:experts, :] = b1_in[...].astype(F32)

time: 283 us -> 283 us (level)
  no operation moved by 1% of the time
where the time goes in v4:
time: 283 us; the launch traced here: 282 us
  Pallas kernels  281 us (99%)
    pallas_call x1, Pallas kernels, per_device(): pl.pallas_call(functools.partial(block_kernel, fsdp, experts), out_shape=...  275 us
    pallas_call x1, Pallas kernels, per_device(): pl.pallas_call(functools.partial(finish_kernel, own, experts), out_shape=...  5.74 us

profile of v4, /device:TPU:0, one launch (start us, length us, event | category | flops | bytes accessed | tf_op | source)
XLA Modules:
  0.0 282.0 jit_solution(16256243024150274167)
XLA Ops:
  0.7 275.4 %block.1 = (f32[2,200,768]{2,1,0:T(8,128)}, f32[2,200,768]{2,1,0:T(8,128)}, f32[3,96,192]{2,1,0:T(8,128)}, f32[96,192]{1,0:T(8,128)}, f32[4,96,768]{2,1,0:T(8,12...) custom-call(s32[2,4]{1,0:T(2,128)} %refs_0_.1, bf16[2,200,768]{2,1,0:T(8,128)(2,1)} %refs_1_.1, ...), custom_call_target="tpu_custom_call" | custom-call | tf_op jit(solution)/shard_map/block/pallas_call | solution.py:936
  276.0 5.7 %finish.1 = (f32[1,96]{1,0:T(1,128)}, f32[1,96]{1,0:T(1,128)}, f32[1,96]{1,0:T(1,128)}, f32[1,96]{1,0:T(1,128)}, f32[1,96]{1,0:T(1,128)}, /*index=5*/f32[4,96]{1...) custom-call(f32[24,768]{1,0:T(8,128)} %get-tuple-element.35.refs_0_,, ...), custom_call_target="tpu_custom_call" | custom-call | tf_op jit(solution)/shard_map/finish/pallas_call | solution.py:1012

commit v5 on v4

--- a/solution.py
+++ b/solution.py
@@ -306,7 +306,7 @@
     small_out, r2 = take(2)
     rowsb, dyg, rin, qkv, prob, mix, hid, awg, par, parg = take(10)
     wbuf, part, first, second, r1, a1, a2 = take(7)
-    hot_s, gts, xs, vs, gas, dps, sid, rp, dmx, hb, ob, b1 = take(12)
+    hot_s, gts, xs, vs, gas, dps, sid, rp, dmx, hb, ob, b1, r2_last = take(13)
     z1, z2, z3, z4, zs = take(5)
     ga = take(4)
     rs = take(4)
@@ -343,9 +343,19 @@
     gat_par = Gather(net, lambda j: parg.at[j], ga, 0)
     gat_aw = Gather(net, lambda j: awg.at[j], ga, 1)
     gat = lambda e: Gather(net, lambda j: wbuf.at[e, j], ga, 2 + e)
-    red_e = lambda e: Reduce(
-        net, lambda j: wbuf.at[e, j], lambda k: r1.at[e, k], lambda k: r2.at[e, k], rs, e, fetch
-    )
+    def red_e(e):
+        final = e == experts - 1
+        second_of = lambda k: r2_last.at[k - 1] if final else r2.at[e, k]
+        return Reduce(
+            net,
+            lambda j: wbuf.at[e, j],
+            lambda k: r1.at[e, k],
+            second_of,
+            rs,
+            e,
+            None if final else fetch,
+        )
+
     red_a = Reduce(net, lambda j: awg.at[j], lambda k: a1.at[k], lambda k: a2.at[k], rs, experts)
 
     def row_gather(buf, m, unit):
@@ -819,7 +829,6 @@
     red_e(2).collect()
     expert_out(2)
     red_a.middle(steps)
-    red_e(3).collect()
     expert_out(3)
     made = red_a.finish()
     for c in range(3):
@@ -979,6 +988,7 @@
             vmem((8, ff), F32),
             vmem((8, width), F32),
             vmem((8, ff), F32),
+            vmem((half - 1, 2, own, ff)),
             vmem((16, width), F32),
             vmem((16, width), F32),
             vmem((24, width), F32),

time: 283 us -> 283 us (level)
  no operation moved by 1% of the time
where the time goes in v5:
time: 283 us; the launch traced here: 282 us
  Pallas kernels  281 us (99%)
    pallas_call x1, Pallas kernels, per_device(): pl.pallas_call(functools.partial(block_kernel, fsdp, experts), out_shape=...  275 us
    pallas_call x1, Pallas kernels, per_device(): pl.pallas_call(functools.partial(finish_kernel, own, experts), out_shape=...  5.74 us

profile of v5, /device:TPU:0, one launch (start us, length us, event | category | flops | bytes accessed | tf_op | source)
XLA Modules:
  0.0 282.0 jit_solution(6641702219829044894)
XLA Ops:
  0.7 275.4 %block.1 = (f32[2,200,768]{2,1,0:T(8,128)}, f32[2,200,768]{2,1,0:T(8,128)}, f32[3,96,192]{2,1,0:T(8,128)}, f32[96,192]{1,0:T(8,128)}, f32[4,96,768]{2,1,0:T(8,12...) custom-call(s32[2,4]{1,0:T(2,128)} %refs_0_.1, bf16[2,200,768]{2,1,0:T(8,128)(2,1)} %refs_1_.1, ...), custom_call_target="tpu_custom_call" | custom-call | tf_op jit(solution)/shard_map/block/pallas_call | solution.py:945
  276.0 5.7 %finish.1 = (f32[1,96]{1,0:T(1,128)}, f32[1,96]{1,0:T(1,128)}, f32[1,96]{1,0:T(1,128)}, f32[1,96]{1,0:T(1,128)}, f32[1,96]{1,0:T(1,128)}, /*index=5*/f32[4,96]{1...) custom-call(f32[24,768]{1,0:T(8,128)} %get-tuple-element.35.refs_0_,, ...), custom_call_target="tpu_custom_call" | custom-call | tf_op jit(solution)/shard_map/finish/pallas_call | solution.py:1022
